TPU v7x, 32 devices: a whole 2x2x4 slice. The times are simulated.
32 devices in a mesh: ctx: 8 (over z, y), fsdp: 4 (over x, core).
Axes of the slice: x: 2, y: 2, z: 4, core: 2. Of those that a mesh axis runs over, the one named last changes fastest.
Arguments:
- tokens: bfloat16 [12, 512, 2048], P('fsdp', 'ctx'), may hold values from -6 to 6
- lengths: int32 [12], P('fsdp'), may hold values from 128 to 512, as said below
- norm_gains: float32 [2, 2048], replicated, may hold values from 0.24 to 1.8
- attention_weight: float32 [2048, 6144], P(('ctx', 'fsdp'))
- feed_weight: float32 [2048, 24576], P(('ctx', 'fsdp'))
- cotangent: bfloat16 [12, 512, 2048], P('fsdp', 'ctx'), may hold values from -7.5 to 7.5
- attention_mean: float32 [2048, 6144], P(('ctx', 'fsdp'))
- attention_square: float32 [2048, 6144], P(('ctx', 'fsdp')), as said below
- feed_mean: float32 [2048, 24576], P(('ctx', 'fsdp'))
- feed_square: float32 [2048, 24576], P(('ctx', 'fsdp')), as said below
- gain_mean: float32 [2, 2048], replicated
- gain_square: float32 [2, 2048], replicated, as said below
Outputs:
- layer_output: bfloat16 [12, 512, 2048], P('fsdp', 'ctx')
- input_gradient: float32 [12, 512, 2048], P('fsdp', 'ctx')
- gradient_norm: float32 [], replicated
- attention_master: float32 [2048, 6144], P(('ctx', 'fsdp'))
- attention_means: float32 [2048, 6144], P(('ctx', 'fsdp'))
- attention_squares: float32 [2048, 6144], P(('ctx', 'fsdp'))
- attention_copy: bfloat16 [2048, 6144], P(('ctx', 'fsdp'))
- feed_master: float32 [2048, 24576], P(('ctx', 'fsdp'))
- feed_means: float32 [2048, 24576], P(('ctx', 'fsdp'))
- feed_squares: float32 [2048, 24576], P(('ctx', 'fsdp'))
- feed_copy: bfloat16 [2048, 24576], P(('ctx', 'fsdp'))
- gains_updated: float32 [2, 2048], replicated
- gains_means: float32 [2, 2048], replicated
- gains_squares: float32 [2, 2048], replicated
Inputs may be any that keep to these rules, and one draw needn't show every extreme that they name: `lengths`: of the 3 consecutive sequences on one index of fsdp, one has length 512. `attention_square`: positive. `feed_square`: positive. `gain_square`: positive.
All inputs are finite; a program needn't handle non-finite values.
Results may differ from a plain program's by a relative error of at most 0.013.
Values may be sent and summed in bfloat16 or wider, within the bound.
A program may use at most 896 MiB of HBM per device.

v0:
```python
import functools

import jax
import jax.numpy as jnp
from jax import lax
from jax.experimental import pallas as pl
from jax.experimental.pallas import tpu as pltpu
from jax.sharding import Mesh, PartitionSpec as P

QUERY_HEADS = 8
KEY_VALUE_HEADS = 4
HEAD_SIZE = 256
FF = 8192
STEP = 10

norm_eps = 1e-06
rope_base = 1000042.0
masked_value = -1e30
clip_norm = 1.0
beta_one = 0.9
beta_two = 0.95
adam_eps = 1e-08
matrix_rate = 0.03
gain_rate = 0.4
weight_decay = 0.1

TEAM = ("y", "x", "c")
ALL = ("z", "y", "x", "c")


MESH = pl.DeviceIdType.MESH
VMEM = pl.BlockSpec(memory_space=pltpu.VMEM)
HBM = pl.BlockSpec(memory_space=pl.ANY)


def place():
    y, x, c = lax.axis_index("y"), lax.axis_index("x"), lax.axis_index("c")
    return y, x, c, lambda yy, xx, cc: (yy * 2 + xx) * 2 + cc


def hail(others):
    barrier = pltpu.get_barrier_semaphore()
    for other in others:
        pl.semaphore_signal(barrier, inc=1, device_id=other, device_id_type=MESH)
    return lambda: pl.semaphore_wait(barrier, len(others))


def greet(others):
    hail(others)()


def gather_kernel(src, *refs):
    out, send, recv, own = refs[-4:]
    y, x, c, index = place()
    to_x, to_y, to_s = {"x": 1 - x}, {"y": 1 - y}, {"c": 1 - c}
    me, at_x, at_y, at_d = index(y, x, c), index(y, 1 - x, c), index(1 - y, x, c), index(1 - y, 1 - x, c)
    half = src.shape[0] // 2
    rows = (pl.ds(0, half), pl.ds(half, half))
    local = pltpu.make_async_copy(src, out.at[me], own)
    local.start()
    greet((to_x, to_y, to_s))

    def hop(slot, block, part, where, first=False):
        piece = out.at[block, rows[part]]
        return pltpu.make_async_remote_copy(
            src_ref=src.at[rows[part]] if first else piece,
            dst_ref=piece,
            send_sem=send.at[slot],
            recv_sem=recv.at[slot],
            device_id=where,
            device_id_type=MESH,
        )

    x0, x1 = hop(0, me, 0, to_x, True), hop(1, me, 1, to_x, True)
    y1, y0 = hop(2, me, 1, to_y, True), hop(3, me, 0, to_y, True)
    s0, s1 = hop(4, me, 0, to_s, True), hop(5, me, 1, to_s, True)
    for copy in (x0, y1, x1, y0, s0, s1):
        copy.start()
    x0.wait_recv()
    d0 = hop(6, at_x, 0, to_y)
    d0.start()
    y1.wait_recv()
    d1 = hop(7, at_y, 1, to_x)
    d1.start()
    sx0, sy1 = hop(8, at_x, 0, to_s), hop(9, at_y, 1, to_s)
    sx0.start()
    sy1.start()
    x1.wait_recv()
    sx1 = hop(10, at_x, 1, to_s)
    sx1.start()
    y0.wait_recv()
    sy0 = hop(11, at_y, 0, to_s)
    sy0.start()
    d0.wait_recv()
    sd0 = hop(12, at_d, 0, to_s)
    sd0.start()
    d1.wait_recv()
    sd1 = hop(13, at_d, 1, to_s)
    sd1.start()
    for copy in (s0, s1, sx0, sy1, sx1, sy0, sd0, sd1):
        copy.wait_recv()
    for copy in (x0, x1, y0, y1, s0, s1, d0, d1, sx0, sy1, sx1, sy0, sd0, sd1):
        copy.wait_send()
    local.wait()


def plane_gather(value, number, after=()):
    return pl.pallas_call(
        gather_kernel,
        out_shape=jax.ShapeDtypeStruct((8, *value.shape), value.dtype),
        in_specs=[HBM] * (1 + len(after)),
        out_specs=HBM,
        scratch_shapes=[
            pltpu.SemaphoreType.DMA((14,)),
            pltpu.SemaphoreType.DMA((14,)),
            pltpu.SemaphoreType.DMA,
        ],
        compiler_params=pltpu.CompilerParams(collective_id=number, has_side_effects=True),
        cost_estimate=pl.CostEstimate(flops=1, bytes_accessed=1, transcendentals=0),
        name="plane_gather",
    )(value, *after)


def sum_kernel(lefts, terms, tile, *refs):
    a_refs, w_refs = refs[:lefts], refs[lefts : lefts + len(terms)]
    out, s_send, s_recv, d_send, d_recv, x_send, x_recv, y_send, y_recv, x_acc, y_acc, send, recv = refs[-13:]
    y, x, c, index = place()
    to_x, to_y, to_s = {"x": 1 - x}, {"y": 1 - y}, {"c": 1 - c}
    rows, width = out.shape
    half = rows // 2
    parts = (pl.ds(0, half), pl.ds(half, half))
    f32, low = jnp.float32, jnp.bfloat16

    def product(block, put):
        lines = pl.ds(pl.multiple_of(block * rows, rows), rows)

        @pl.loop(0, width // tile)
        def _(step):
            cols = pl.ds(pl.multiple_of(step * tile, tile), tile)
            total = None
            for (left, start), w_ref in zip(terms, w_refs):
                term = mm_nt(a_refs[left][lines, start : start + w_ref.shape[1]], w_ref[cols, :])
                total = term if total is None else total + term
            put(cols, total)

    def hop(slot, src, dst, where):
        copy = pltpu.make_async_remote_copy(
            src_ref=src, dst_ref=dst, send_sem=send.at[slot], recv_sem=recv.at[slot],
            device_id=where, device_id_type=MESH,
        )
        return copy

    def to_sibling(slot, yy, xx):
        def put(cols, total):
            s_send[slot, :, cols] = total.astype(low)

        product(index(yy, xx, 1 - c), put)
        copy = hop(slot, s_send.at[slot], s_recv.at[slot], to_s)
        copy.start()
        return copy

    def with_sibling(slot, yy, xx, keep):
        def put(cols, total):
            keep[:, cols] = (total + s_recv[slot, :, cols].astype(f32)).astype(keep.dtype)

        product(index(yy, xx, c), put)

    greet((to_x, to_y, to_s))
    s0 = to_sibling(0, 1 - y, 1 - x)
    s1 = to_sibling(1, y, 1 - x)
    s0.wait_recv()
    with_sibling(0, 1 - y, 1 - x, d_send)
    d0 = hop(4, d_send.at[parts[0]], d_recv.at[parts[0]], to_x)
    d1 = hop(5, d_send.at[parts[1]], d_recv.at[parts[1]], to_y)
    d0.start()
    d1.start()
    s1.wait_recv()
    with_sibling(1, y, 1 - x, x_acc)
    x_send[parts[0]] = x_acc[parts[0]].astype(low)
    x0 = hop(6, x_send.at[parts[0]], x_recv.at[parts[0]], to_x)
    x0.start()
    s2 = to_sibling(2, 1 - y, x)
    s2.wait_recv()
    with_sibling(2, 1 - y, x, y_acc)
    y_send[parts[1]] = y_acc[parts[1]].astype(low)
    y1 = hop(7, y_send.at[parts[1]], y_recv.at[parts[1]], to_y)
    y1.start()
    s3 = to_sibling(3, y, x)
    d1.wait_recv()
    x_send[parts[1]] = (x_acc[parts[1]] + d_recv[parts[1]].astype(f32)).astype(low)
    x1 = hop(8, x_send.at[parts[1]], x_recv.at[parts[1]], to_x)
    x1.start()
    d0.wait_recv()
    y_send[parts[0]] = (y_acc[parts[0]] + d_recv[parts[0]].astype(f32)).astype(low)
    y0 = hop(9, y_send.at[parts[0]], y_recv.at[parts[0]], to_y)
    y0.start()
    s3.wait_recv()
    with_sibling(3, y, x, out)
    x0.wait_recv()
    y1.wait_recv()
    x1.wait_recv()
    y0.wait_recv()
    out[...] += x_recv[...].astype(f32) + y_recv[...].astype(f32)
    for copy in (s0, s1, s2, s3, d0, d1, x0, x1, y0, y1):
        copy.wait_send()


def plane_sum(lefts, rights, number, after=(), tile=512):
    ends = [(left, start) for left, a in enumerate(lefts) for start in range(0, a.shape[1], rights[0].shape[1])]
    terms = tuple(ends[: len(rights)])
    rows, width = lefts[0].shape[0] // 8, rights[0].shape[0]
    block = (rows, width)
    low, f32 = jnp.bfloat16, jnp.float32
    return pl.pallas_call(
        functools.partial(sum_kernel, len(lefts), terms, min(tile, width)),
        out_shape=jax.ShapeDtypeStruct(block, f32),
        in_specs=[VMEM] * (len(lefts) + len(rights)) + [HBM] * len(after),
        out_specs=VMEM,
        scratch_shapes=[
            pltpu.VMEM((4, *block), low),
            pltpu.VMEM((4, *block), low),
            *[pltpu.VMEM(block, low)] * 6,
            pltpu.VMEM(block, f32),
            pltpu.VMEM(block, f32),
            pltpu.SemaphoreType.DMA((10,)),
            pltpu.SemaphoreType.DMA((10,)),
        ],
        compiler_params=pltpu.CompilerParams(
            collective_id=number, has_side_effects=True, vmem_limit_bytes=48 * 2**20
        ),
        cost_estimate=pl.CostEstimate(flops=1, bytes_accessed=1, transcendentals=0),
        name="plane_sum",
    )(*lefts, *rights, *after)


def swap_kernel(pieces, takes, *refs):
    count = len(pieces)
    sources, (send, recv, own) = refs[: -2 * count - 3], refs[-3:]
    outs, holds = refs[-2 * count - 3 : -count - 3], refs[-count - 3 : -3]
    y, x, c, index = place()
    me = index(y, x, c)
    flips = [(fy, fx, fc) for fy, fx in ((1, 1), (0, 1), (1, 0), (0, 0)) for fc in (0, 1)]
    flips = [flip for flip in flips if flip != (0, 0, 0)]

    def there(flip):
        return tuple(1 - at if f else at for at, f in zip((y, x, c), flip))

    greet([dict(zip(("y", "x", "c"), there(flip))) for flip in flips])
    copies = []
    for piece in range(count):
        for number, flip in enumerate(flips):
            yy, xx, cc = there(flip)
            member = index(yy, xx, cc)
            holds[piece][number] = takes[piece](sources, member, cc)
            copy = pltpu.make_async_remote_copy(
                src_ref=holds[piece].at[number],
                dst_ref=outs[piece].at[me],
                send_sem=send.at[piece * 7 + number],
                recv_sem=recv.at[piece * 7 + number],
                device_id={"y": yy, "x": xx, "c": cc},
                device_id_type=MESH,
            )
            copy.start()
            copies.append(copy)
        holds[piece][7] = takes[piece](sources, me, c)
        keep = pltpu.make_async_copy(holds[piece].at[7], outs[piece].at[me], own.at[piece])
        keep.start()
        copies.append(keep)
    for copy in copies:
        copy.wait()


def plane_swap(sources, shapes, takes, number, after=()):
    low = jnp.bfloat16
    count = len(shapes)
    return pl.pallas_call(
        functools.partial(swap_kernel, shapes, takes),
        out_shape=[jax.ShapeDtypeStruct((8, *shape), low) for shape in shapes],
        in_specs=[VMEM] * len(sources) + [HBM] * len(after),
        out_specs=[HBM] * count,
        scratch_shapes=[
            *[pltpu.VMEM((8, *shape), low) for shape in shapes],
            pltpu.SemaphoreType.DMA((7 * count,)),
            pltpu.SemaphoreType.DMA((7 * count,)),
            pltpu.SemaphoreType.DMA((count,)),
        ],
        compiler_params=pltpu.CompilerParams(
            collective_id=number, has_side_effects=True, vmem_limit_bytes=48 * 2**20
        ),
        cost_estimate=pl.CostEstimate(flops=1, bytes_accessed=1, transcendentals=0),
        name="plane_swap",
    )(*sources, *after)


def team_of(y, x, c):
    flips = [(fy, fx, fc) for fy, fx in ((1, 1), (0, 1), (1, 0), (0, 0)) for fc in (0, 1)]
    return [
        tuple(1 - at if f else at for at, f in zip((y, x, c), flip)) for flip in flips if flip != (0, 0, 0)
    ]


def turn_kernel(planes, src, *refs):
    y, x, c, index = place()
    me = index(y, x, c)
    others = team_of(y, x, c)
    ids = [dict(zip(("y", "x", "c"), other)) for other in others]
    if planes:
        out, total, near, far, held, send, recv, own, send_lines, recv_lines = refs[-10:]
        z = lax.axis_index("z")
        column = [{"z": lax.rem(z + step, planes)} for step in range(1, planes)]
        fetch = pltpu.make_async_copy(src, held, own.at[1])
        fetch.start()
    else:
        out, send, recv, own = refs[-4:]
        column = []
    ready = hail(ids + column)
    if planes:
        fetch.wait()
        squares = jnp.zeros((8, held.shape[1]), jnp.float32)
        for start in range(0, held.shape[0], 64):
            part = held[start : start + 64].astype(jnp.float32)
            squares += jnp.sum(jnp.square(part).reshape(8, 8, -1), axis=0)
        near[me] = jnp.broadcast_to(jnp.sum(squares, keepdims=True), near.shape[1:])
    ready()
    count = src.shape[0] // 8

    def rows(member):
        return src.at[pl.ds(pl.multiple_of(member * count, count), count)]

    def spread(buffer, at, where, base):
        copies = [
            pltpu.make_async_remote_copy(
                src_ref=buffer.at[at],
                dst_ref=buffer.at[at],
                send_sem=send_lines.at[base + number],
                recv_sem=recv_lines.at[base + number],
                device_id=other,
                device_id_type=MESH,
            )
            for number, other in enumerate(where)
        ]
        for copy in copies:
            copy.start()
        return copies

    copies = [
        pltpu.make_async_remote_copy(
            src_ref=rows(index(*other)),
            dst_ref=out.at[me],
            send_sem=send.at[number],
            recv_sem=recv.at[number],
            device_id=where,
            device_id_type=MESH,
        )
        for number, (other, where) in enumerate(zip(others, ids))
    ]
    copies.append(pltpu.make_async_copy(rows(me), out.at[me], own.at[0]))
    small = spread(near, me, ids, 0) if planes else []
    for copy in copies:
        copy.start()
    if planes:
        for copy in small:
            copy.wait()
        far[z] = jnp.sum(near[...], axis=0)
        for copy in spread(far, z, column, 7):
            copy.wait()
        total[...] = jnp.sum(far[...], axis=0)
    for copy in copies:
        copy.wait()


def total_kernel(planes, src, *refs):
    out, near, far, send, recv = refs[-5:]
    y, x, c, index = place()
    z = lax.axis_index("z")
    ids = [dict(zip(("y", "x", "c"), other)) for other in team_of(y, x, c)]
    column = [{"z": lax.rem(z + step, planes)} for step in range(1, planes)]
    me = index(y, x, c)
    near[me] = src[...]
    greet(ids + column)

    def spread(buffer, at, where, base):
        copies = [
            pltpu.make_async_remote_copy(
                src_ref=buffer.at[at],
                dst_ref=buffer.at[at],
                send_sem=send.at[base + number],
                recv_sem=recv.at[base + number],
                device_id=other,
                device_id_type=MESH,
            )
            for number, other in enumerate(where)
        ]
        for copy in copies:
            copy.start()
        for copy in copies:
            copy.wait()

    spread(near, me, ids, 0)
    far[z] = jnp.sum(near[...], axis=0)
    spread(far, z, column, 7)
    out[...] = jnp.sum(far[...], axis=0)


def total_sum(value, planes, number, after=()):
    return pl.pallas_call(
        functools.partial(total_kernel, planes),
        out_shape=jax.ShapeDtypeStruct(value.shape, value.dtype),
        in_specs=[VMEM] + [HBM] * len(after),
        out_specs=VMEM,
        scratch_shapes=[pltpu.VMEM((size, *value.shape), value.dtype) for size in (8, planes)]
        + [pltpu.SemaphoreType.DMA((6 + planes,))] * 2,
        compiler_params=pltpu.CompilerParams(
            collective_id=number, has_side_effects=True, vmem_limit_bytes=16 * 2**20
        ),
        cost_estimate=pl.CostEstimate(flops=1, bytes_accessed=1, transcendentals=0),
        name="total_sum",
    )(value, *after)


def turn(rows, number, after=(), planes=0):
    block = (rows.shape[0] // 8, rows.shape[1])
    dma = pltpu.SemaphoreType.DMA
    out_shape, out_specs = [jax.ShapeDtypeStruct((8, *block), rows.dtype)], [HBM]
    scratch = [dma((7,)), dma((7,)), dma((2,))]
    if planes:
        tile = jax.ShapeDtypeStruct((8, 128), jnp.float32)
        out_shape.append(tile)
        out_specs.append(VMEM)
        buffers = [pltpu.VMEM((size, *tile.shape), tile.dtype) for size in (8, planes)]
        scratch = buffers + [pltpu.VMEM(rows.shape, rows.dtype)] + scratch + [dma((6 + planes,)), dma((6 + planes,))]
    return pl.pallas_call(
        functools.partial(turn_kernel, planes),
        out_shape=out_shape,
        in_specs=[HBM] * (1 + len(after)),
        out_specs=out_specs,
        scratch_shapes=scratch,
        compiler_params=pltpu.CompilerParams(
            collective_id=number, has_side_effects=True, vmem_limit_bytes=56 * 2**20
        ),
        cost_estimate=pl.CostEstimate(flops=1, bytes_accessed=1, transcendentals=0),
        name="turn",
    )(rows, *after)


def hops(planes, send, recv, block, up):
    z = lax.axis_index("z")

    def step(number):
        gone, came = (z - number + 1, z - number) if up else (z + number - 1, z + number)
        goes = ((gone >= 0) & (z + 1 < planes)) if up else ((gone < planes) & (z >= 1))
        comes = (came >= 0) if up else (came < planes)

        def copy(b):
            return pltpu.make_async_remote_copy(
                src_ref=block(b),
                dst_ref=block(b),
                send_sem=send.at[number - 1],
                recv_sem=recv.at[number - 1],
                device_id={"z": z + 1 if up else z - 1},
                device_id_type=MESH,
            )

        return (
            lambda: pl.when(goes)(lambda: copy(gone).start()),
            lambda: pl.when(comes)(lambda: copy(came).wait_recv()),
            lambda: pl.when(goes)(lambda: copy(gone).wait_send()),
        )

    return [step(number) for number in range(1, planes)]


def ring(planes):
    z = lax.axis_index("z")
    return [{"z": lax.rem(z + 1, planes)}, {"z": lax.rem(z + planes - 1, planes)}]


def spread_to(others, ids, source, take, hold, place_of, send, recv, own, ready=None):
    y, x, c, index = place()
    me = index(y, x, c)
    copies = []
    if ready is not None:
        for number, other in enumerate(others):
            hold[number] = take([source], index(*other), other[2])
        ready()
    for number, (other, where) in enumerate(zip(others, ids)):
        if ready is None:
            hold[number] = take([source], index(*other), other[2])
        copy = pltpu.make_async_remote_copy(
            src_ref=hold.at[number], dst_ref=place_of(me), send_sem=send.at[number], recv_sem=recv.at[number],
            device_id=where, device_id_type=MESH,
        )
        copy.start()
        copies.append(copy)
    hold[7] = take([source], me, c)
    keep = pltpu.make_async_copy(hold.at[7], place_of(me), own)
    keep.start()
    return copies, keep


def begin_kernel(
    planes, take, take_feed, attention, feed, tokens_from, gain, all_attention, all_rows, columns,
    tokens, held, hold, feed_held, feed_hold, rows, a_send, a_recv, f_send, f_recv, r_send, r_recv, u_send, u_recv, d_send, d_recv, own,
):
    y, x, c, index = place()
    z = lax.axis_index("z")
    me, at_x, at_y, at_d = index(y, x, c), index(y, 1 - x, c), index(1 - y, x, c), index(1 - y, 1 - x, c)
    others = team_of(y, x, c)
    ids = [dict(zip(("y", "x", "c"), other)) for other in others]
    to_x, to_y, to_s = {"x": 1 - x}, {"y": 1 - y}, {"c": 1 - c}
    count = held.shape[0]
    half = rows.shape[0] // 2
    parts = (pl.ds(0, half), pl.ds(half, half))
    fetch = pltpu.make_async_copy(attention, held, own.at[0])
    fetch.start()
    fetch_tokens = pltpu.make_async_copy(tokens_from, tokens, own.at[5])
    fetch_tokens.start()
    fetch_feed = pltpu.make_async_copy(feed.at[:, pl.ds(0, feed_held.shape[1])], feed_held, own.at[3])
    fetch_feed.start()
    ready = hail(ids + ring(planes))
    fetch.wait()

    def attention_rows(start, size):
        return all_attention.at[pl.ds(pl.multiple_of(start, count), size)]

    a_copies, a_keep = spread_to(
        others, ids, held, take, hold, lambda m: attention_rows((z * 8 + m) * count, count), a_send, a_recv, own.at[1], ready
    )

    def hop(slot, block, part, where, first=False):
        piece = all_rows.at[block, parts[part]]
        copy = pltpu.make_async_remote_copy(
            src_ref=rows.at[parts[part]] if first else piece, dst_ref=piece,
            send_sem=r_send.at[slot], recv_sem=r_recv.at[slot], device_id=where, device_id_type=MESH,
        )
        copy.start()
        return copy

    for copy in a_copies:
        copy.wait_recv()
    a_keep.wait()

    def plane_block(b):
        return attention_rows(b * 8 * count, 8 * count)

    up = hops(planes, u_send, u_recv, plane_block, True)
    down = hops(planes, d_send, d_recv, plane_block, False)

    def pass_on(number):
        if number > 0:
            up[number - 1][1]()
            down[number - 1][1]()
        if number < planes - 1:
            up[number][0]()
            down[number][0]()

    pass_on(0)
    fetch_tokens.wait()

    @pl.loop(0, rows.shape[0] // 16)
    def _(group):
        lines = pl.ds(pl.multiple_of(group * 16, 16), 16)
        rows[lines] = rms_forward(tokens[lines].astype(jnp.float32), gain[...])[0].astype(rows.dtype)

    x0, y1 = hop(0, me, 0, to_x, True), hop(2, me, 1, to_y, True)
    x1, y0 = hop(1, me, 1, to_x, True), hop(3, me, 0, to_y, True)
    s0, s1 = hop(4, me, 0, to_s, True), hop(5, me, 1, to_s, True)
    mine = pltpu.make_async_copy(rows, all_rows.at[me], own.at[2])
    mine.start()
    x0.wait_recv()
    d0 = hop(6, at_x, 0, to_y)
    y1.wait_recv()
    d1 = hop(7, at_y, 1, to_x)
    sx0, sy1 = hop(8, at_x, 0, to_s), hop(9, at_y, 1, to_s)
    fetch_feed.wait()
    f_copies, f_keep = spread_to(
        others, ids, feed_held, take_feed, feed_hold, lambda m: columns.at[m], f_send, f_recv, own.at[4]
    )
    pass_on(1)
    x1.wait_recv()
    sx1 = hop(10, at_x, 1, to_s)
    y0.wait_recv()
    sy0 = hop(11, at_y, 0, to_s)
    pass_on(2)
    d0.wait_recv()
    sd0 = hop(12, at_d, 0, to_s)
    d1.wait_recv()
    sd1 = hop(13, at_d, 1, to_s)
    for number in range(3, planes):
        pass_on(number)
    for copy in (s0, s1, sx0, sy1, sx1, sy0, sd0, sd1, *f_copies):
        copy.wait_recv()
    for copy in (x0, x1, y0, y1, s0, s1, d0, d1, sx0, sy1, sx1, sy0, sd0, sd1, *a_copies, *f_copies):
        copy.wait_send()
    for step in up + down:
        step[2]()
    mine.wait()
    f_keep.wait()


def begin(attention, feed, tokens, gain, takes, widths, planes, number):
    low, dma = jnp.bfloat16, pltpu.SemaphoreType.DMA
    count = attention.shape[0]
    return pl.pallas_call(
        functools.partial(begin_kernel, planes, *takes),
        out_shape=[
            jax.ShapeDtypeStruct((planes * 8 * count, widths[0]), low),
            jax.ShapeDtypeStruct((8, *tokens.shape), low),
            jax.ShapeDtypeStruct((8, count, widths[1]), low),
        ],
        in_specs=[HBM, HBM, HBM, VMEM],
        out_specs=[HBM] * 3,
        scratch_shapes=[
            pltpu.VMEM(tokens.shape, tokens.dtype),
            pltpu.VMEM(attention.shape, attention.dtype),
            pltpu.VMEM((8, count, widths[0]), low),
            pltpu.VMEM((count, 8 * widths[1]), feed.dtype),
            pltpu.VMEM((8, count, widths[1]), low),
            pltpu.VMEM(tokens.shape, low),
            *[dma((size,)) for size in (7, 7, 7, 7, 14, 14, *[planes - 1] * 4, 6)],
        ],
        compiler_params=pltpu.CompilerParams(
            collective_id=number, has_side_effects=True, vmem_limit_bytes=54 * 2**20
        ),
        cost_estimate=pl.CostEstimate(flops=1, bytes_accessed=1, transcendentals=0),
        name="begin",
    )(attention, feed, tokens, gain)


def turned(value, cos_table, sin_table):
    half = value.shape[1] // 2
    first, second = value[:, :half], value[:, half:]
    return jnp.concatenate([first * cos_table - second * sin_table, second * cos_table + first * sin_table], axis=1)


def climb_kernel(
    planes, rows, weights, cos, sin, mine, other, weight, held, zeros, stay, u_send, u_recv, s_send, s_recv, own, fill, move
):
    z, c = lax.axis_index("z"), lax.axis_index("c")
    to_s = {"c": 1 - c}
    barrier = pltpu.get_barrier_semaphore()
    for where in [to_s] + ring(planes):
        pl.semaphore_signal(barrier, inc=1, device_id=where, device_id_type=MESH)
    count, (sides, span) = rows.shape[0], cos.shape[:2]
    size = 512
    pull_weight = pltpu.make_async_copy(
        weights.at[:, pl.ds(weight.shape[1], weight.shape[1])], weight, move.at[count // size]
    )
    pull_weight.start()
    pulls = [
        pltpu.make_async_copy(rows.at[pl.ds(start, size)], held.at[pl.ds(start, size)], move.at[start // size])
        for start in range(0, count, size)
    ]
    for copy in pulls:
        copy.start()
    pull_weight.wait()
    for start in range(0, count, size):
        pulls[start // size].wait()
        value = mm(held[start : start + size], weight[...])
        for line in range(0, size, span):
            side = (start + line) // (count // sides)
            part = value[line : line + span]
            part = jnp.where(c == 0, turned(part, cos[side], sin[side]), part)
            stay[start + line : start + line + span] = part.astype(stay.dtype)
    zeros[...] = jnp.zeros_like(zeros)
    pl.semaphore_wait(barrier, 3)

    def across(n):
        return pltpu.make_async_remote_copy(
            src_ref=stay if n == 0 else mine.at[n], dst_ref=other.at[n], send_sem=s_send.at[n], recv_sem=s_recv.at[n],
            device_id=to_s, device_id_type=MESH,
        )

    def along(n):
        return pltpu.make_async_remote_copy(
            src_ref=stay if n == 1 else mine.at[n - 1], dst_ref=mine.at[n], send_sem=u_send.at[n - 1], recv_sem=u_recv.at[n - 1],
            device_id={"z": z + 1}, device_id_type=MESH,
        )

    def fills(n):
        return [
            pltpu.make_async_copy(zeros, buffer.at[n], fill.at[2 * (n - 1) + number])
            for number, buffer in enumerate((mine, other))
        ]

    keep = pltpu.make_async_copy(stay, mine.at[0], own)
    more = z + 1 < planes
    pl.when(more)(lambda: along(1).start())
    across(0).start()
    keep.start()
    for n in range(1, planes):

        @pl.when(z < n)
        def _():
            for copy in fills(n):
                copy.start()

    for n in range(1, planes):

        @pl.when(z >= n)
        def _():
            along(n).wait_recv()
            if n + 1 < planes:
                pl.when(more)(lambda: along(n + 1).start())
            across(n).start()

    across(0).wait()
    keep.wait()
    for n in range(1, planes):

        @pl.when(z >= n)
        def _():
            across(n).wait()

        @pl.when(z < n)
        def _():
            for copy in fills(n):
                copy.wait()

        pl.when((z >= n - 1) & more)(lambda: along(n).wait_send())


def climb(rows, weights, cos, sin, planes, number):
    dma = pltpu.SemaphoreType.DMA
    block = (rows.shape[0], weights.shape[1] // 3)
    blocks = jax.ShapeDtypeStruct((planes, *block), rows.dtype)
    return pl.pallas_call(
        functools.partial(climb_kernel, planes),
        out_shape=[blocks, blocks],
        in_specs=[HBM] * 2 + [VMEM] * 2,
        out_specs=[HBM] * 2,
        scratch_shapes=[
            pltpu.VMEM((weights.shape[0], block[1]), rows.dtype),
            pltpu.VMEM(rows.shape, rows.dtype),
            pltpu.VMEM(block, rows.dtype),
            pltpu.VMEM(block, rows.dtype),
            *[dma((size,)) for size in (planes - 1, planes - 1, planes, planes)],
            dma,
            dma((2 * (planes - 1),)),
            dma((rows.shape[0] // 512 + 1,)),
        ],
        compiler_params=pltpu.CompilerParams(
            collective_id=number, has_side_effects=True, vmem_limit_bytes=56 * 2**20
        ),
        cost_estimate=pl.CostEstimate(flops=1, bytes_accessed=1, transcendentals=0),
        name="climb",
    )(rows, weights, cos, sin)


def fall_kernel(
    planes, terms_from, rows, left_from, query_term, out_term, cos, sin, value, term, blocks,
    terms, left, sends, recvs, total, first, held, send, recv, t_send, t_recv, own, move, fetch,
):
    y, x, c, index = place()
    z = lax.axis_index("z")
    me = index(y, x, c)
    others = team_of(y, x, c)
    ids = [dict(zip(("y", "x", "c"), other)) for other in others]
    f32 = jnp.float32
    count = rows.shape[0] // 8
    size = terms.shape[2]
    given = ((query_term, 0), (out_term, 2))
    pulls = [pltpu.make_async_copy(ref, held.at[n], move.at[n]) for n, (ref, _) in enumerate(given)]
    get_terms = pltpu.make_async_copy(terms_from, terms, fetch.at[0])
    get_terms.start()
    get_left = pltpu.make_async_copy(left_from, left, fetch.at[1])
    get_left.start()
    for copy in pulls:
        copy.start()
    greet(ids + ring(planes))
    get_terms.wait()

    def rows_of(member):
        return rows.at[pl.ds(pl.multiple_of(member * count, count), count)]

    half = terms.shape[1] // 2
    parts = [pl.ds(n * half, half) for n in range(2)]

    def hop(step, n):
        slot = 2 * (step - 1) + n
        return pltpu.make_async_remote_copy(
            src_ref=sends.at[step - 1, parts[n]], dst_ref=recvs.at[step - 1, parts[n]],
            send_sem=send.at[slot], recv_sem=recv.at[slot], device_id={"z": z - 1}, device_id_type=MESH,
        )

    def came(step):
        return (z + 1 < planes) & (z + 1 + step - planes >= 0)

    copies = [
        pltpu.make_async_remote_copy(
            src_ref=rows_of(index(*other)), dst_ref=blocks.at[me], send_sem=t_send.at[number], recv_sem=t_recv.at[number],
            device_id=where, device_id_type=MESH,
        )
        for number, (other, where) in enumerate(zip(others, ids))
    ]
    copies.append(pltpu.make_async_copy(rows_of(me), blocks.at[me], own))
    pushes = []
    for step in range(1, planes):
        block = z + step - planes
        for n in range(2):
            lines = parts[n]
            if step > 1:
                pl.when(came(step - 1))(lambda: hop(step - 1, n).wait_recv())

            @pl.when((block >= 0) & (z + 1 == planes))
            def _():
                sends[step - 1, lines] = terms[block, lines]

            if step > 1:

                @pl.when((block >= 0) & (z + 1 < planes))
                def _():
                    added = terms[block, lines].astype(f32) + recvs[step - 2, lines].astype(f32)
                    sends[step - 1, lines] = added.astype(terms.dtype)

            pl.when(block >= 0)(lambda: hop(step, n).start())
        if step == 1:
            for copy in copies:
                copy.start()
            total[...] = terms[z].astype(f32)
            for n, (_, column) in enumerate(given):
                pulls[n].wait()
                pushes.append(
                    pltpu.make_async_copy(held.at[n], term.at[:, pl.ds(column * size, size)], move.at[2 + n])
                )
                pushes[-1].start()
    last = planes - 1
    sides, span = cos.shape[:2]
    get_left.wait()
    for n in range(2):
        lines = parts[n]

        @pl.when(came(last))
        def _():
            hop(last, n).wait_recv()
            total[lines] += recvs[last - 1, lines].astype(f32)

        for line in range(n * half, (n + 1) * half, span):
            side = line // (total.shape[0] // sides)
            part = total[line : line + span]
            part = jnp.where(c == 0, turned(part, cos[side], -sin[side]), part)
            value[line : line + span] = part.astype(value.dtype)
        upright = value[lines].astype(f32).T.astype(value.dtype)
        for start in range(0, left.shape[1], 512):
            columns = pl.ds(start, 512)
            made = mm(upright, left[lines, columns])
            if n == 0:
                first[:, columns] = made
                continue
            held[2, columns] = (first[:, columns] + made).T.astype(held.dtype)
            pushes.append(
                pltpu.make_async_copy(
                    held.at[2, columns], term.at[columns, pl.ds(size, size)], move.at[4 + start // 512]
                )
            )
            pushes[-1].start()
    for step in range(1, planes):
        for n in range(2):
            pl.when(z + step - planes >= 0)(lambda: hop(step, n).wait_send())
    for copy in copies + pushes:
        copy.wait()


def fall(terms, rows, left, query_term, out_term, cos, sin, planes, number):
    block = terms.shape[1:]
    dma, low = pltpu.SemaphoreType.DMA, terms.dtype
    return pl.pallas_call(
        functools.partial(fall_kernel, planes),
        out_shape=[
            jax.ShapeDtypeStruct(block, low),
            jax.ShapeDtypeStruct((left.shape[1], 3 * block[1]), low),
            jax.ShapeDtypeStruct((8, rows.shape[0] // 8, rows.shape[1]), low),
        ],
        in_specs=[HBM] * 5 + [VMEM] * 2,
        out_specs=[VMEM, HBM, HBM],
        scratch_shapes=[pltpu.VMEM(terms.shape, low), pltpu.VMEM(left.shape, low)]
        + [pltpu.VMEM((planes - 1, *block), low)] * 2
        + [pltpu.VMEM(block, jnp.float32), pltpu.VMEM((block[1], left.shape[1]), jnp.float32)]
        + [pltpu.VMEM((3, left.shape[1], block[1]), low)]
        + [dma((2 * (planes - 1),))] * 2
        + [dma((7,)), dma((7,)), dma, dma((4 + left.shape[1] // 512,)), dma((2,))],
        compiler_params=pltpu.CompilerParams(
            collective_id=number, has_side_effects=True, vmem_limit_bytes=56 * 2**20
        ),
        cost_estimate=pl.CostEstimate(flops=1, bytes_accessed=1, transcendentals=0),
        name="fall",
    )(terms, rows, left, query_term, out_term, cos, sin)


def dot(left, right, contract):
    return lax.dot_general(left, right, (contract, ((), ())), preferred_element_type=jnp.float32)


def mm(left, right):
    return dot(left, right, ((1,), (0,)))


def mm_nt(left, right):
    return dot(left, right, ((1,), (1,)))


def mm_tn(left, right):
    return dot(left, right, ((0,), (0,)))


def bmm(pattern, left, right):
    return jnp.einsum(pattern, left, right, preferred_element_type=jnp.float32)


def angle_tables(positions):
    half_dim = HEAD_SIZE // 2
    frequency = rope_base ** (-(jnp.arange(half_dim).astype(jnp.float32) * 2.0) / HEAD_SIZE)
    phases = positions.astype(jnp.float32)[:, None] * frequency[None, :]
    return (jnp.cos(phases), jnp.sin(phases))


def rotate(value, cos_table, sin_table):
    half = value.shape[-1] // 2
    a, b = value[..., :half], value[..., half:]
    return jnp.concatenate([a * cos_table - b * sin_table, b * cos_table + a * sin_table], axis=-1)


def rms_forward(value, gain_row):
    inverse = lax.rsqrt(jnp.mean(value * value, axis=-1, keepdims=True) + norm_eps)
    return (value * inverse * gain_row, inverse)


def rms_back(grad_out, value, inverse, gain_row):
    scaled = grad_out * gain_row
    grad_in = inverse * (
        scaled - value * inverse * inverse * jnp.mean(scaled * value, axis=-1, keepdims=True)
    )
    return (grad_in, jnp.sum(grad_out * value * inverse, axis=0))


def adamw(weight, gradient, moment_one, moment_two, step_rate, decay_rate, invert=jnp.reciprocal):
    mean_new = beta_one * moment_one + (1.0 - beta_one) * gradient
    square_new = beta_two * moment_two + (1.0 - beta_two) * gradient * gradient
    below = jnp.sqrt(square_new * (1.0 / (1.0 - beta_two**STEP))) + adam_eps
    direction = mean_new * (1.0 / (1.0 - beta_one**STEP)) * invert(below)
    return (weight - step_rate * (direction + decay_rate * weight), mean_new, square_new)


def attention_parts(core, length, q_ref, mine_ref, other_ref, query_ref, key_ref):
    mine, other = mine_ref[...].reshape(-1, HEAD_SIZE), other_ref[...].reshape(-1, HEAD_SIZE)
    first = core == 0
    k, v = jnp.where(first, mine, other), jnp.where(first, other, mine)
    q = q_ref[...].reshape(-1, HEAD_SIZE)
    at, key_at = query_ref[...], key_ref[...]
    allowed = (key_at <= at) & (key_at < length) & (key_at >= 0)
    scores = jnp.where(allowed, mm_nt(q, k) * HEAD_SIZE ** (-0.5), masked_value)
    exponent = jnp.exp(scores - jnp.max(scores, axis=-1, keepdims=True))
    return q, k, v, exponent / jnp.sum(exponent, axis=-1, keepdims=True)


def attention_kernel(core_ref, length_ref, q_ref, mine_ref, other_ref, query_ref, key_ref, out_ref):
    length = length_ref[pl.program_id(0)]
    _, _, v, soft = attention_parts(core_ref[0], length, q_ref, mine_ref, other_ref, query_ref, key_ref)
    out_ref[...] = mm(soft.astype(jnp.bfloat16), v).astype(jnp.bfloat16).reshape(out_ref.shape)


def attention_back_kernel(
    core_ref, length_ref, q_ref, mine_ref, other_ref, query_ref, key_ref, do_ref, cos_ref, sin_ref,
    dq_ref, keep_ref, send_ref,
):
    low = jnp.bfloat16
    core = core_ref[0]
    length = length_ref[pl.program_id(0)]
    q, k, v, soft = attention_parts(core, length, q_ref, mine_ref, other_ref, query_ref, key_ref)
    do = do_ref[...].reshape(-1, HEAD_SIZE)
    dp = mm_nt(do, v)
    delta = jnp.sum(soft * dp, axis=-1, keepdims=True)
    ds = (soft * (dp - delta) * HEAD_SIZE ** (-0.5)).astype(low)
    dq = mm(ds, k)
    cos_table, sin_table = cos_ref[...], sin_ref[...]
    half = HEAD_SIZE // 2
    a, b = dq[:, :half], dq[:, half:]
    turned = jnp.concatenate([a * cos_table + b * sin_table, b * cos_table - a * sin_table], axis=-1)
    dq_ref[...] = turned.astype(low).reshape(dq_ref.shape)
    dk, dv = mm_tn(ds, q), mm_tn(soft.astype(low), do)
    first = core == 0
    keep, send = (t.reshape(keep_ref.shape) for t in (jnp.where(first, dk, dv), jnp.where(first, dv, dk)))
    for block in range(keep_ref.shape[0]):
        at = core_ref[1 + block]
        keep_ref[at] = keep[block]
        send_ref[at] = send[block].astype(low)


def attention_call(kernel, core, lengths, q, mine, other, query_pos, key_pos, extra, outs, name):
    ny, count, span, size = q.shape
    nz = mine.shape[0]
    rows = pl.BlockSpec((ny, 1, span, size), lambda i, *_: (0, i, 0, 0))
    keys = pl.BlockSpec((nz, ny, 1, span, size), lambda i, *_: (0, 0, i, 0, 0))

    def whole(value):
        return pl.BlockSpec(value.shape, lambda i, *_: (0,) * value.ndim)

    kinds = {"rows": (rows, q.shape), "keys": (keys, mine.shape)}
    return pl.pallas_call(
        kernel,
        grid_spec=pltpu.PrefetchScalarGridSpec(
            num_scalar_prefetch=2,
            grid=(count,),
            in_specs=[rows, keys, keys, whole(query_pos), whole(key_pos)]
            + [rows if value.shape == q.shape else whole(value) for value in extra],
            out_specs=[kinds[kind][0] for kind, _ in outs],
        ),
        out_shape=[jax.ShapeDtypeStruct(kinds[kind][1], dtype) for kind, dtype in outs],
        compiler_params=pltpu.CompilerParams(vmem_limit_bytes=48 * 2**20),
        cost_estimate=pl.CostEstimate(flops=1, bytes_accessed=1, transcendentals=0),
        name=name,
    )(core, lengths, q, mine, other, query_pos, key_pos, *extra)


def feed_back_kernel(dyb_ref, weight_ref, gate_ref, up_ref, out_ref):
    dm = mm(dyb_ref[...], weight_ref[...])
    gate, upward = gate_ref[...], up_ref[...]
    sig = jax.nn.sigmoid(gate)
    part = gate.shape[1]
    out_ref[:, :part] = (dm * upward * sig * (1.0 + gate * (1.0 - sig))).astype(out_ref.dtype)
    out_ref[:, part:] = (dm * gate * sig).astype(out_ref.dtype)


def feed_back(dyb, weight, both, lines=256):
    count, part = both.shape[0], both.shape[1] // 2

    def rows(width, column=0):
        return pl.BlockSpec((lines, width), lambda i: (i, column))

    return pl.pallas_call(
        feed_back_kernel,
        grid=(count // lines,),
        in_specs=[rows(dyb.shape[1]), pl.BlockSpec(weight.shape, lambda i: (0, 0)), rows(part), rows(part, 1)],
        out_specs=rows(2 * part),
        out_shape=jax.ShapeDtypeStruct((count, 2 * part), jnp.bfloat16),
        compiler_params=pltpu.CompilerParams(vmem_limit_bytes=48 * 2**20),
        cost_estimate=pl.CostEstimate(flops=1, bytes_accessed=1, transcendentals=0),
        name="feed_back",
    )(dyb, weight, both, both)


def close_reciprocal(value):
    guess = pltpu.reciprocal(value, approx=True)
    return guess * (2.0 - value * guess)


def norm_of(lines_ref, tile_ref):
    gains = lines_ref[:-8]
    return jnp.sqrt(jnp.sum(gains * gains, keepdims=True) + lines_ref[-8:-7, 0:1] + tile_ref[0:1, 0:1])


def update_kernel(*refs):
    lines_ref, tile_ref, gain_ref, gate_up_ref, down_ref, attention_ref = refs[:6]
    gains, feed, attention = refs[6:9], refs[9:12], refs[12:15]
    new_gains, norm_ref, new_feed, new_attention, factor_ref = refs[15:18], refs[18], refs[19:23], refs[23:27], refs[27]
    rows = feed[0].shape[0]
    lines = pl.ds(pl.multiple_of(pl.program_id(0) * rows, rows), rows)

    @pl.when(pl.program_id(0) == 0)
    def _():
        norm = norm_of(lines_ref, tile_ref)
        norm_ref[...] = norm
        factor_ref[...] = clip_norm / norm
        weight, mean, square = (ref[...] for ref in gains)
        gradient = gain_ref[...] * factor_ref[...]
        for ref, value in zip(new_gains, adamw(weight, gradient, mean, square, gain_rate, 0.0)):
            ref[...] = value

    factor = factor_ref[...]

    def piece(olds, news, grad_ref, member, start, column, size):
        at = pl.ds(pl.multiple_of(column, size), size)
        gradient = grad_ref[member, lines, pl.ds(start, size)].astype(jnp.float32) * factor
        weight, mean, square = (ref[:, at] for ref in olds)
        values = adamw(weight, gradient, mean, square, matrix_rate, weight_decay, close_reciprocal)
        for ref, value in zip(news, (*values, values[0])):
            ref[:, at] = value.astype(ref.dtype)

    part = down_ref.shape[2]
    size = min(part, 512)

    @pl.loop(0, 8)
    def _(member):
        for offset in range(0, part, size):
            for number, (grad_ref, start) in enumerate(((gate_up_ref, 0), (gate_up_ref, part), (down_ref, 0))):
                column = (number * 8 + member) * part + offset
                piece(feed, new_feed, grad_ref, member, start + offset, column, size)
        core = lax.rem(member, 2)
        kv_column = (8 + 4 * core + lax.div(member, 2)) * HEAD_SIZE
        for number, column in enumerate((member * HEAD_SIZE, kv_column, (16 + member) * HEAD_SIZE)):
            piece(attention, new_attention, attention_ref, member, number * HEAD_SIZE, column, HEAD_SIZE)


def update(sums, grads, gains, feed, attention):
    f32, low = jnp.float32, jnp.bfloat16
    rows = min(feed[0].shape[0], 16)

    def some(value):
        return pl.BlockSpec((rows, value.shape[1]), lambda i: (i, 0))

    def whole(value):
        return pl.BlockSpec(value.shape, lambda i: (0,) * value.ndim)

    norm = jax.ShapeDtypeStruct((1, 1), f32)
    matrices = [jax.ShapeDtypeStruct(part[0].shape, dtype) for part in (feed, attention) for dtype in (f32, f32, f32, low)]
    return pl.pallas_call(
        update_kernel,
        grid=(feed[0].shape[0] // rows,),
        in_specs=[whole(value) for value in (*sums, *grads, *gains)] + [some(value) for value in (*feed, *attention)],
        out_specs=[whole(value) for value in (*gains, norm)] + [some(value) for value in matrices],
        out_shape=[jax.ShapeDtypeStruct(gains[0].shape, f32)] * 3 + [norm] + matrices,
        scratch_shapes=[pltpu.VMEM((1, 1), f32)],
        compiler_params=pltpu.CompilerParams(vmem_limit_bytes=56 * 2**20),
        name="update",
    )(*sums, *grads, *gains, *feed, *attention)


def is_square():
    return lax.axis_size("y") == 2 and lax.axis_size("x") == 2


def swap(blocks):
    return lax.all_to_all(blocks, TEAM, split_axis=0, concat_axis=0, tiled=True)


def over_planes(blocks):
    return lax.all_gather(blocks.reshape(-1, blocks.shape[-1]), "z", axis=0, tiled=True)


def scatter_planes(term):
    return lax.psum_scatter(term, "z", scatter_dimension=0, tiled=True)


def together(*values):
    return lax.optimization_barrier(values)


def scatter_team(rows, number, after=()):
    if not is_square():
        return swap(rows.reshape(8, -1, rows.shape[-1]))
    return turn(rows, number, after)[0]


def team_gather(local, number, after=()):
    if not is_square():
        return lax.all_gather(local, TEAM, axis=0, tiled=True)
    return plane_gather(local, number, after).reshape(-1, local.shape[1])


def team_sum(lefts, rights, number, after=()):
    if is_square():
        return plane_sum(lefts, rights, number, after)
    partial = mm_nt(jnp.concatenate(lefts, axis=1), jnp.concatenate(rights, axis=1))
    return lax.psum_scatter(partial.astype(jnp.bfloat16), TEAM, scatter_dimension=0, tiled=True).astype(jnp.float32)


def local(
    tokens,
    lengths,
    norm_gains,
    attention_weight,
    feed_weight,
    cotangent,
    attention_mean,
    attention_square,
    feed_mean,
    feed_square,
    gain_mean,
    gain_square,
):
    low = jnp.bfloat16
    sequences, span, width = tokens.shape
    ny, nx, nz = lax.axis_size("y"), lax.axis_size("x"), lax.axis_size("z")
    team = ny * nx * 2
    core = lax.axis_index("c")
    rows = attention_weight.shape[0]
    q_width, kv_width = QUERY_HEADS * HEAD_SIZE, KEY_VALUE_HEADS * HEAD_SIZE
    count = sequences * span
    all_sequences = nx * 2 * sequences
    reach = ny * span
    near = is_square()
    ff_part = FF // team

    def columns(start, size):
        return pl.ds(pl.multiple_of(start, size), size)

    def take_attention(sources, member, c):
        source = sources[0]
        starts = (
            member * HEAD_SIZE,
            q_width + c * kv_width + (member - c) // 2 * HEAD_SIZE,
            q_width + 2 * kv_width + member * HEAD_SIZE,
        )
        return jnp.concatenate([source[:, columns(s, HEAD_SIZE)].astype(low) for s in starts], axis=1)

    def take_feed(*parts):
        return lambda sources, member, c: jnp.concatenate(
            [sources[0][:, columns(part * FF + member * ff_part, ff_part)].astype(low) for part in parts], axis=1
        )

    def spread(source, take, size, number, after=()):
        if is_square():
            blocks = plane_swap([source], [(rows, size)], [take], number, after)[0]
        else:
            blocks = swap(jnp.stack([take([source], member, member % 2) for member in range(8)]))
        return blocks, over_planes(blocks)

    team_base = lax.axis_index("z") * reach
    team_pos = team_base + jnp.arange(reach, dtype=jnp.int32)
    own_pos = team_base + lax.axis_index("y") * span + jnp.arange(span, dtype=jnp.int32)
    if near:
        key_pos = jnp.concatenate([team_pos - back * reach for back in range(nz)])
    else:
        key_pos = jnp.arange(nz * reach, dtype=jnp.int32)
    query_at, key_at = team_pos[:, None], key_pos[None, :]
    cos_table, sin_table = angle_tables(team_pos)
    cos_rows, sin_rows = (t.reshape(ny, 1, span, -1) for t in (cos_table, sin_table))
    valid = (own_pos[None, :] < lengths[:, None]).astype(jnp.float32).reshape(count, 1)
    lengths_all = lax.all_gather(lengths, ("x", "c"), axis=0, tiled=True)
    planes = jnp.arange(nz, dtype=jnp.int32)
    if near:
        planes = (lax.axis_index("z") - planes) % nz
    core_at = jnp.concatenate([jnp.reshape(core, (1,)), planes]).astype(jnp.int32)

    def heads(value):
        return value.reshape(ny, all_sequences, span, HEAD_SIZE)

    x_in = tokens.reshape(count, width).astype(jnp.float32)
    normed_one, inverse_one = rms_forward(x_in, norm_gains[0])
    outer_grad = cotangent.reshape(count, width).astype(jnp.float32) * valid
    if is_square():
        attention_mine, h1, gate_up_blocks = begin(
            attention_weight,
            feed_weight,
            tokens.reshape(count, width),
            norm_gains[:1],
            (take_attention, take_feed(0, 1)),
            (3 * HEAD_SIZE, 2 * ff_part),
            nz,
            1,
        )
        h1 = h1.reshape(-1, width)
    else:
        attention_mine = spread(attention_weight, take_attention, 3 * HEAD_SIZE, 1)[1]
        gate_up_blocks, gate_up_weight = spread(feed_weight, take_feed(0, 1), 2 * ff_part, 2)
        h1 = team_gather(normed_one.astype(low), 3)
    query_weight = attention_mine[:, :HEAD_SIZE]
    kv_weight = attention_mine[:, HEAD_SIZE : 2 * HEAD_SIZE]
    out_weight = attention_mine[:, 2 * HEAD_SIZE :]
    tables = [t.reshape(ny, span, -1) for t in (cos_table, sin_table)]
    if is_square():
        kv, other = climb(h1, attention_mine, *tables, nz, 2)
        kv, other = (t.reshape(nz, ny, all_sequences, span, HEAD_SIZE) for t in (kv, other))
        gate_up_blocks, kv = together(gate_up_blocks, kv)
        gate_up_weight = over_planes(gate_up_blocks)
    else:
        kv_raw = heads(mm(h1, kv_weight))
        kv = jnp.where(core == 0, rotate(kv_raw, cos_rows, sin_rows), kv_raw).astype(low)
        kv = lax.all_gather(kv, "z", axis=0, tiled=False)
        other = lax.ppermute(kv, "c", [(0, 1), (1, 0)])
    q = rotate(heads(mm(h1, query_weight)), cos_rows, sin_rows).astype(low)
    attend = (core_at, lengths_all, q, kv, other, query_at, key_at)
    (o,) = attention_call(attention_kernel, *attend, (), [("rows", low)], "attention")
    o = o.reshape(-1, HEAD_SIZE)
    r = x_in + team_sum([o], [out_weight], 4)

    normed_two, inverse_two = rms_forward(r, norm_gains[1])
    h2 = team_gather(normed_two.astype(low), 16)
    dyb = team_gather(outer_grad.astype(low), 15, [h2])
    down_blocks, down_weight = spread(feed_weight, take_feed(2), ff_part, 12, [dyb])
    gate_up_weight, down_blocks = together(gate_up_weight, down_blocks)
    both = mm(h2, gate_up_weight)
    gate, upward = both[:, :ff_part], both[:, ff_part:]
    sig = jax.nn.sigmoid(gate)
    m = (gate * sig * upward).astype(low)
    down_term = mm_tn(dyb, m).astype(low)
    down_rows = scatter_planes(down_term)
    down_weight, down_term = together(down_weight, down_term)
    d_both = feed_back(dyb, down_weight, both)
    gate_up_term = mm_tn(h2, d_both).astype(low)
    gate_up_rows = scatter_planes(gate_up_term)
    dh2 = team_sum([d_both], [gate_up_weight], 7, [gate_up_term, down_term])
    mid_grad, gain_two = rms_back(dh2, r, inverse_two, norm_gains[1])
    dr = outer_grad + mid_grad
    drb = team_gather(dr.astype(low), 13, [down_rows])

    do = heads(mm(drb, out_weight).astype(low))
    dq, keep, theirs = attention_call(
        attention_back_kernel,
        *attend,
        (do, cos_table, sin_table),
        [("rows", low), ("keys", jnp.float32), ("keys", low)],
        "attention_back",
    )
    dq = dq.reshape(-1, HEAD_SIZE)
    dkv = keep + lax.ppermute(theirs, "c", [(0, 1), (1, 0)]).astype(jnp.float32)
    low_terms = dkv.astype(low)
    feed_sum = team_sum([m], [down_weight], 5, [low_terms])
    down_grad = scatter_team(down_rows, 6, [low_terms])
    layer_output = (r + feed_sum).astype(low)
    local_squares = sum(jnp.sum(jnp.square(part.astype(jnp.float32))) for part in (gate_up_rows, down_rows))
    query_term, out_term = mm_tn(h1, dq).astype(low), mm_tn(drb, o).astype(low)
    low_terms, gate_up_rows, layer_output, down_grad, query_term, out_term = together(
        low_terms, gate_up_rows, layer_output, down_grad, query_term, out_term
    )
    if is_square():
        low_terms = low_terms.reshape(nz, -1, HEAD_SIZE)
        dkv, attention_term, gate_up_grad = fall(low_terms, gate_up_rows, h1, query_term, out_term, *tables, nz, 8)
    else:
        dkv = lax.psum_scatter(low_terms, "z", scatter_dimension=0, tiled=True)[0].astype(jnp.float32)
        dkv = jnp.where(core == 0, rotate(dkv, cos_rows, -sin_rows), dkv).astype(low).reshape(-1, HEAD_SIZE)
        attention_term = jnp.concatenate([query_term, mm_tn(h1, dkv).astype(low), out_term], axis=1)
        gate_up_grad = scatter_team(gate_up_rows, 8)
    attention_rows = scatter_planes(attention_term)
    dh1 = team_sum([dq, dkv], [query_weight, kv_weight], 9, [attention_term])
    in_grad, gain_one = rms_back(dh1, x_in, inverse_one, norm_gains[0])
    input_gradient = dr + in_grad
    gain_local = jnp.stack([gain_one, gain_two]).reshape(-1, 128)
    lines = jnp.concatenate([gain_local, jnp.full((8, 128), local_squares)], axis=0)
    if is_square():
        lines = total_sum(lines, nz, 18)
        attention_grad, tile = turn(attention_rows, 10, (), nz)
    else:
        lines = lax.psum(lines, ALL)
        attention_grad = scatter_team(attention_rows, 10)
        tile = lax.psum(jnp.full((8, 128), jnp.sum(jnp.square(attention_rows.astype(jnp.float32)))), ALL)
    gain_grad = lines[:-8].reshape(2, width)
    news = update(
        (lines, tile, gain_grad),
        (gate_up_grad, down_grad, attention_grad),
        (norm_gains, gain_mean, gain_square),
        (feed_weight, feed_mean, feed_square),
        (attention_weight, attention_mean, attention_square),
    )
    gains_new, gradient_norm, feed_new, attention_new = news[:3], news[3], news[4:8], news[8:]
    return (
        layer_output.reshape(sequences, span, width),
        input_gradient.reshape(sequences, span, width),
        gradient_norm.reshape(()),
        *attention_new,
        *feed_new,
        *gains_new,
    )


def solution(mesh):
    ctx, fsdp = mesh.shape["ctx"], mesh.shape["fsdp"]
    inner = QUERY_HEADS // fsdp
    fine = Mesh(mesh.devices.reshape(ctx // inner, inner, fsdp // 2, 2), ALL)
    act = P(("x", "c"), ("z", "y"), None)
    matrix = P(ALL, None)
    return jax.shard_map(
        local,
        mesh=fine,
        in_specs=(act, P(("x", "c")), P(), matrix, matrix, act, matrix, matrix, matrix, matrix, P(), P()),
        out_specs=(act, act, P(), matrix, matrix, matrix, matrix, matrix, matrix, matrix, matrix, P(), P(), P()),
        check_vma=False,
    )
```

profile of v0, /device:TPU:1, one launch (start us, length us, event | category | flops | bytes accessed | tf_op | source)
XLA Modules:
  0.0 760.0 jit_solution(15707318163164213327)
XLA Ops:
  9.6 71.3 %begin.1 = (bf16[2048,768]{1,0:T(8,128)(2,1)}, bf16[8,192,2048]{2,1,0:T(8,128)(2,1)}, bf16[8,64,2048]{2,1,0:T(8,128)(2,1)}) custom-call(f32[64,6144]{1,0:T(8,128)} %refs_12_.1, f32[64,24576]{1,0:T(8,128)} %refs_9_.1, bf16[192,2048]{1,0:T(8,128)(2,1)} %bitcast.61, f32[1,2048]{1,0:T(1,128)} %get-tuple-element.100.gain), custom_call_target="tpu_custom_call" | custom-call | flops 1 | bytes 1 | tf_op jit(solution)/shard_map/begin/pallas_call | solution.py:604
  80.9 21.6 %climb.1 = (bf16[4,1536,256]{2,1,0:T(8,128)(2,1)}, bf16[4,1536,256]{2,1,0:T(8,128)(2,1)}) custom-call(bf16[1536,2048]{1,0:T(8,128)(2,1)} %bitcast.67, bf16[2048,768]{1,0:T(8,128)(2,1)} %get-tuple-element.51.weights, f32[2,64,128]{2,1,0:T(8,128)} %get-tuple-element.101.cos, f32[2,64,128]{2,1,0:T(8,128)} %get-tuple-element.102.sin), custom_call_target="tpu_custom_call" | custom-call | flops 1 | bytes 1 | tf_op jit(solution)/shard_map/climb/pallas_call | solution.py:727
  117.7 10.5 %attention.3 = bf16[2,12,64,256]{3,2,1,0:T(8,128)(2,1)S(1)} custom-call(s32[5]{0:T(128)S(1)} %pad_add_fusion.1.core_ref, s32[12]{0:T(128)S(1)} %all-reduce.1.length_ref, bf16[2,12,64,256]{3,2,1,0:T(8,128)(2,1)S(1)} %pad_maximum_fusion.q_ref, bf16[4,2,12,64,256]{4,3,2,1,0:T(8,128)(2,1)S(1)} %bitcast.49, bf16[4,2,12,64,256]{4,3,2,1,0:T(8,128)(2,1)} %bitcast.73, ...), custom_call_target="tpu_custom_call" | custom-call | flops 1 | bytes 1 | tf_op jit(solution)/shard_map/attention/pallas_call | solution.py:999
  129.8 33.4 %plane_sum.4 = f32[192,2048]{1,0:T(8,128)S(1)} custom-call(bf16[1536,256]{1,0:T(8,128)(2,1)S(1)} %bitcast.50, bf16[2048,256]{1,0:T(8,128)(2,1)S(1)} %get-tuple-element.95.refs_1_), custom_call_target="tpu_custom_call" | custom-call | flops 1 | bytes 1 | tf_op jit(solution)/shard_map/plane_sum/pallas_call | solution.py:214
  165.7 31.1 %plane_gather.3 = bf16[8,192,2048]{2,1,0:T(8,128)(2,1)} custom-call(bf16[192,2048]{1,0:T(8,128)(2,1)} %multiply_convert_fusion.src), custom_call_target="tpu_custom_call" | custom-call | flops 1 | bytes 1 | tf_op jit(solution)/shard_map/plane_gather/pallas_call | solution.py:108
  198.1 31.1 %plane_gather.4 = bf16[8,192,2048]{2,1,0:T(8,128)(2,1)} custom-call(bf16[192,2048]{1,0:T(8,128)(2,1)} %fusion.10.src, bf16[1536,2048]{1,0:T(8,128)(2,1)} %bitcast.64), custom_call_target="tpu_custom_call" | custom-call | flops 1 | bytes 1 | tf_op jit(solution)/shard_map/plane_gather/pallas_call | solution.py:108
  229.2 17.8 %plane_swap.1 = bf16[8,64,1024]{2,1,0:T(8,128)(2,1)} custom-call(f32[64,24576]{1,0:T(8,128)} %refs_9_.1, bf16[1536,2048]{1,0:T(8,128)(2,1)} %bitcast.57), custom_call_target="tpu_custom_call" | custom-call | flops 1 | bytes 1 | tf_op jit(solution)/shard_map/plane_swap/pallas_call | solution.py:276
  247.2 43.1 %all-gather.5.cloned.1.call-done.refs_1_ = bf16[2048,2048]{1,0:T(8,128)(2,1)} async-done(((bf16[512,2048]{1,0:T(8,128)(2,1)}), bf16[2048,2048]{1,0:T(8,128)(2,1)}) %all-gather.5.cloned.1.call-update) | async-done | bytes 8388624 | tf_op jit(solution)/shard_map/all_gather | solution.py:1127
  290.3 17.3 %fusion.21.gate_ref.up_ref = f32[1536,2048]{1,0:T(8,128)S(1)} fusion(bf16[1536,2048]{1,0:T(8,128)(2,1)} %bitcast.65, bf16[2048,2048]{1,0:T(8,128)(2,1)} %all-gather.5.cloned.1.call-done.refs_1_), kind=kOutput, calls=%fused_computation.66 | convolution fusion | flops 12884901888 | bytes 27262976 | tf_op jit(solution)/shard_map/dot_general | solution.py:891
  314.9 8.5 %convolution_convert_fusion.1.refs_3_ = bf16[2048,1024]{1,0:T(8,128)(2,1)} fusion(bf16[1536,2048]{1,0:T(8,128)(2,1)S(1)} %bitcast.59, bf16[1536,1024]{1,0:T(8,128)(2,1)S(1)} %fusion.refs_0_), kind=kOutput, calls=%fused_computation.5 | convolution fusion | flops 6444548096 | bytes 13631488 | tf_op jit(solution)/shard_map/dot_general | solution.py:891
  323.7 47.0 %all-gather.3.cloned.1.call-done.weight_ref.refs_1_ = bf16[2048,1024]{1,0:T(8,128)(2,1)} async-done(((bf16[512,1024]{1,0:T(8,128)(2,1)}), bf16[2048,1024]{1,0:T(8,128)(2,1)}) %all-gather.3.cloned.1.call-update) | async-done | bytes 4194320 | tf_op jit(solution)/shard_map/all_gather | solution.py:1127
  372.9 14.0 %feed_back.1.refs_0_ = bf16[1536,2048]{1,0:T(8,128)(2,1)} custom-call(bf16[1536,2048]{1,0:T(8,128)(2,1)} %bitcast.58, bf16[2048,1024]{1,0:T(8,128)(2,1)S(1)} %copy-done, f32[1536,2048]{1,0:T(8,128)} %copy-done.13, f32[1536,2048]{1,0:T(8,128)} %copy-done.13), custom_call_target="tpu_custom_call" | custom-call | flops 1 | bytes 1 | tf_op jit(solution)/shard_map/feed_back/pallas_call | solution.py:1030
  386.9 19.4 %convolution_convert_fusion.refs_2_ = bf16[2048,2048]{1,0:T(8,128)(2,1)} fusion(bf16[1536,2048]{1,0:T(8,128)(2,1)} %bitcast.66, bf16[1536,2048]{1,0:T(8,128)(2,1)} %feed_back.1.refs_0_), kind=kOutput, calls=%fused_computation | convolution fusion | flops 12889096192 | bytes 20971520 | tf_op jit(solution)/shard_map/dot_general | solution.py:891
  409.4 49.1 %plane_sum.5 = f32[192,2048]{1,0:T(8,128)S(1)} custom-call(bf16[1536,2048]{1,0:T(8,128)(2,1)} %feed_back.1.refs_0_, bf16[2048,2048]{1,0:T(8,128)(2,1)} %all-gather.5.cloned.1.call-done.refs_1_, bf16[2048,2048]{1,0:T(8,128)(2,1)} %convolution_convert_fusion.refs_2_, bf16[2048,1024]{1,0:T(8,128)(2,1)S(1)} %copy-done.1), custom_call_target="tpu_custom_call" | custom-call | flops 1 | bytes 1 | tf_op jit(solution)/shard_map/plane_sum/pallas_call | solution.py:214
  461.8 31.2 %plane_gather.5 = bf16[8,192,2048]{2,1,0:T(8,128)(2,1)} custom-call(bf16[192,2048]{1,0:T(8,128)(2,1)} %get-tuple-element.90.src, bf16[512,1024]{1,0:T(8,128)(2,1)} %reduce-scatter.4.cloned.1.call-done.refs_0_.src), custom_call_target="tpu_custom_call" | custom-call | flops 1 | bytes 1 | tf_op jit(solution)/shard_map/plane_gather/pallas_call | solution.py:108
  497.9 15.1 %attention_back.1 = (bf16[2,12,64,256]{3,2,1,0:T(8,128)(2,1)S(1)}, f32[4,2,12,64,256]{4,3,2,1,0:T(8,128)}, bf16[4,2,12,64,256]{4,3,2,1,0:T(8,128)(2,1)S(1)}) custom-call(s32[5]{0:T(128)S(1)} %pad_add_fusion.1.core_ref, s32[12]{0:T(128)S(1)} %all-reduce.1.length_ref, bf16[2,12,64,256]{3,2,1,0:T(8,128)(2,1)S(1)} %copy-done.4, ...), custom_call_target="tpu_custom_call" | custom-call | flops 1 | bytes 1 | tf_op jit(solution)/shard_map/attention_back/pallas_call | solution.py:999
  528.8 37.4 %plane_sum.6 = f32[192,2048]{1,0:T(8,128)S(1)} custom-call(bf16[1536,1024]{1,0:T(8,128)(2,1)S(1)} %fusion.refs_0_, bf16[2048,1024]{1,0:T(8,128)(2,1)} %all-gather.3.cloned.1.call-done.weight_ref.refs_1_, bf16[4,2,12,64,256]{4,3,2,1,0:T(8,128)(2,1)} %add_convert_fusion.refs_2_.refs_0_), custom_call_target="tpu_custom_call" | custom-call | flops 1 | bytes 1 | tf_op jit(solution)/shard_map/plane_sum/pallas_call | solution.py:214
  566.2 15.1 %turn.2.refs_4_ = bf16[8,64,1024]{2,1,0:T(8,128)(2,1)} custom-call(bf16[512,1024]{1,0:T(8,128)(2,1)} %reduce-scatter.4.cloned.1.call-done.refs_0_.src, bf16[4,2,12,64,256]{4,3,2,1,0:T(8,128)(2,1)} %add_convert_fusion.refs_2_.refs_0_), custom_call_target="tpu_custom_call" | custom-call | flops 1 | bytes 1 | tf_op jit(solution)/shard_map/turn/pallas_call | solution.py:432
  582.4 13.7 %reduce-scatter.6.cloned.1.call-done.rows = bf16[512,2048]{1,0:T(8,128)(2,1)} async-done(((bf16[2048,2048]{1,0:T(8,128)(2,1)}), bf16[512,2048]{1,0:T(8,128)(2,1)}) %reduce-scatter.6.cloned.1.call-update) | async-done | bytes 2097168 | tf_op jit(solution)/shard_map/reduce_scatter | solution.py:1131
  596.1 44.0 %fall.1 = (bf16[1536,256]{1,0:T(8,128)(2,1)}, bf16[2048,768]{1,0:T(8,128)(2,1)}, bf16[8,64,2048]{2,1,0:T(8,128)(2,1)}) custom-call(bf16[4,1536,256]{2,1,0:T(8,128)(2,1)} %bitcast.60, bf16[512,2048]{1,0:T(8,128)(2,1)} %reduce-scatter.6.cloned.1.call-done.rows, bf16[1536,2048]{1,0:T(8,128)(2,1)} %bitcast.69, ...), custom_call_target="tpu_custom_call" | custom-call | flops 1 | bytes 1 | tf_op jit(solution)/shard_map/fall/pallas_call | solution.py:867
  646.4 35.5 %plane_sum.7 = f32[192,2048]{1,0:T(8,128)S(1)} custom-call(bf16[1536,256]{1,0:T(8,128)(2,1)S(1)} %bitcast.53, bf16[1536,256]{1,0:T(8,128)(2,1)S(1)} %copy-done.11, bf16[2048,256]{1,0:T(8,128)(2,1)S(1)} %copy-done.6, bf16[2048,256]{1,0:T(8,128)(2,1)S(1)} %copy-done.5, bf16[2048,768]{1,0:T(8,128)(2,1)} %get-tuple-element.69.refs_4_), custom_call_target="tpu_custom_call" | custom-call | flops 1 | bytes 1 | tf_op jit(solution)/shard_map/plane_sum/pallas_call | solution.py:214
  687.1 24.9 %total_sum.1.refs_0_ = f32[40,128]{1,0:T(8,128)S(1)} custom-call(f32[40,128]{1,0:T(8,128)S(1)} %concatenate.16.src), custom_call_target="tpu_custom_call" | custom-call | flops 1 | bytes 1 | tf_op jit(solution)/shard_map/total_sum/pallas_call | solution.py:406
  716.3 14.4 %turn.3 = (bf16[8,64,768]{2,1,0:T(8,128)(2,1)}, f32[8,128]{1,0:T(8,128)}) custom-call(bf16[512,768]{1,0:T(8,128)(2,1)} %reduce-scatter.8.cloned.1.call-done.src), custom_call_target="tpu_custom_call" | custom-call | flops 1 | bytes 1 | tf_op jit(solution)/shard_map/turn/pallas_call | solution.py:432
  730.8 22.4 %update.1 = (f32[2,2048]{1,0:T(2,128)}, f32[2,2048]{1,0:T(2,128)}, f32[2,2048]{1,0:T(2,128)}, f32[1,1]{1,0:T(1,128)}, f32[64,24576]{1,0:T(8,128)}, /*index=5*/f3...) custom-call(f32[40,128]{1,0:T(8,128)} %copy-done.12, ...), custom_call_target="tpu_custom_call" | custom-call | tf_op jit(solution)/shard_map/update/pallas_call | solution.py:1106
  (132 shorter events, 74.5 us)
Async XLA Ops:
  7.2 283.2 %all-gather.5.cloned.1.call-start = ((), (), s32[]{:S(2)}) async-start(), calls=%async_computation.4 | async-start | bytes 10485760 | tf_op jit(solution)/shard_map/all_gather | solution.py:1127
  80.9 30.0 %copy-start.22 = (bf16[2048,768]{1,0:T(8,128)(2,1)S(1)}, bf16[2048,768]{1,0:T(8,128)(2,1)}, u32[]{:S(2)}) copy-start(bf16[2048,768]{1,0:T(8,128)(2,1)} %get-tuple-element.51.weights) | copy-start | bytes 9437188
  102.6 268.2 %all-gather.3.cloned.1.call-start = ((), (), s32[]{:S(2)}) async-start(), calls=%async_computation.3 | async-start | bytes 5242880 | tf_op jit(solution)/shard_map/all_gather | solution.py:1127
  110.9 4.7 copy-start.27
  110.9 4.6 copy-start.28
  115.9 12.3 %copy-start.3 = (bf16[2,12,64,256]{3,2,1,0:T(8,128)(2,1)}, bf16[2,12,64,256]{3,2,1,0:T(8,128)(2,1)S(1)}, u32[]{:S(2)}) copy-start(bf16[2,12,64,256]{3,2,1,0:T(8,128)(2,1)S(1)} %pad_maximum_fusion.q_ref) | copy-start | bytes 2359300
  129.8 33.4 %copy-start.18 = (bf16[3,64,2048]{2,1,0:T(8,128)(2,1)S(1)}, bf16[3,64,2048]{2,1,0:T(8,128)(2,1)}, u32[]{:S(2)}) copy-start(bf16[3,64,2048]{2,1,0:T(8,128)(2,1)} %param.12) | copy-start | bytes 2359300
  165.7 31.3 %copy-start.24 = (bf16[3,64,2048]{2,1,0:T(8,128)(2,1)S(1)}, bf16[3,64,2048]{2,1,0:T(8,128)(2,1)}, u32[]{:S(2)}) copy-start(bf16[3,64,2048]{2,1,0:T(8,128)(2,1)} %param.17) | copy-start | bytes 2359300
  247.0 214.8 %reduce-scatter.4.cloned.1.call-start = ((), (), s32[]{:S(2)}) async-start(), calls=%async_computation.5 | async-start | bytes 5242880 | tf_op jit(solution)/shard_map/reduce_scatter | solution.py:1131
  307.6 4.5 copy-start.13
  323.4 272.7 %reduce-scatter.6.cloned.1.call-start = ((), (), s32[]{:S(2)}) async-start(), calls=%async_computation.6 | async-start | bytes 10485760 | tf_op jit(solution)/shard_map/reduce_scatter | solution.py:1131
  406.3 310.0 %reduce-scatter.8.cloned.1.call-start = ((), (), s32[]{:S(2)}) async-start(), calls=%async_computation.7 | async-start | bytes 3932160 | tf_op jit(solution)/shard_map/reduce_scatter | solution.py:1131
  409.4 49.1 %copy-start.16 = (f32[192,2048]{1,0:T(8,128)S(1)}, f32[192,2048]{1,0:T(8,128)}, u32[]{:S(2)}) copy-start(f32[192,2048]{1,0:T(8,128)} %copy-done.15) | copy-start | bytes 4718596
  493.0 4.9 copy-start.4
  497.9 15.4 %copy-start.8 = (bf16[2,12,64,256]{3,2,1,0:T(8,128)(2,1)S(1)}, bf16[2,12,64,256]{3,2,1,0:T(8,128)(2,1)}, u32[]{:S(2)}) copy-start(bf16[2,12,64,256]{3,2,1,0:T(8,128)(2,1)} %copy-done.7) | copy-start | bytes 2359300
  497.9 28.0 %slice-start = ((s8[6291456]{0:T(1024)(128)(4,1)}), s8[4194304]{0:T(1024)(128)(4,1)S(1)}, s32[]{:S(2)}) async-start(s8[6291456]{0:T(1024)(128)(4,1)} %bitcast.70), calls=%async_computation.8 | async-start | bytes 8388608
  513.1 12.8 %copy-start.9 = (bf16[2,12,64,256]{3,2,1,0:T(8,128)(2,1)}, bf16[2,12,64,256]{3,2,1,0:T(8,128)(2,1)S(1)}, u32[]{:S(2)}) copy-start(bf16[2,12,64,256]{3,2,1,0:T(8,128)(2,1)S(1)} %get-tuple-element.62) | copy-start | bytes 2359300
  513.1 12.8 %slice-start.1 = ((s8[6291456]{0:T(1024)(128)(4,1)}), s8[2097152]{0:T(1024)(128)(4,1)S(1)}, s32[]{:S(2)}) async-start(s8[6291456]{0:T(1024)(128)(4,1)} %bitcast.70), calls=%async_computation.9 | async-start | bytes 4194304
  513.1 6.3 collective-permute-start
  513.3 7.7 %copy-start.23 = (f32[4,2,12,64,256]{4,3,2,1,0:T(8,128)S(1)}, f32[4,2,12,64,256]{4,3,2,1,0:T(8,128)}, u32[]{:S(2)}) copy-start(f32[4,2,12,64,256]{4,3,2,1,0:T(8,128)} %get-tuple-element.60) | copy-start | bytes 18874372
  566.2 15.2 %copy-start.17 = (f32[192,2048]{1,0:T(8,128)S(1)}, f32[192,2048]{1,0:T(8,128)}, u32[]{:S(2)}) copy-start(f32[192,2048]{1,0:T(8,128)} %copy-done.15) | copy-start | bytes 4718596
  646.4 35.5 %copy-start.20 = (bf16[3,64,2048]{2,1,0:T(8,128)(2,1)S(1)}, bf16[3,64,2048]{2,1,0:T(8,128)(2,1)}, u32[]{:S(2)}) copy-start(bf16[3,64,2048]{2,1,0:T(8,128)(2,1)} %param.12) | copy-start | bytes 2359300
  646.4 35.5 %copy-start.29 = (f32[1,2048]{1,0:T(1,128)S(1)}, f32[1,2048]{1,0:T(1,128)}, u32[]{:S(2)}) copy-start(f32[1,2048]{1,0:T(1,128)} %get-tuple-element.100.gain) | copy-start | bytes 24580
  681.9 30.8 %copy-start.21 = (bf16[3,64,2048]{2,1,0:T(8,128)(2,1)S(1)}, bf16[3,64,2048]{2,1,0:T(8,128)(2,1)}, u32[]{:S(2)}) copy-start(bf16[3,64,2048]{2,1,0:T(8,128)(2,1)} %param.12) | copy-start | bytes 2359300
  (16 other events, 32.4 us)
Sparse Core Ops, SparseCore 0:
  102.7 187.6 all-gather.4
  291.9 78.7 all-gather.2
  373.6 75.2 reduce-scatter.3
  451.3 144.7 reduce-scatter.5
  640.3 75.9 reduce-scatter.7
where the time goes:
time: 768 us; the launch traced here: 760 us
  Pallas kernels  520 us (68%)
  waiting for transfers between devices  104 us (14%)
  matrix products  63.6 us (8%)
  other arithmetic  24.1 us (3%)
  local copies, waits for them, and re-layouts  23.7 us (3%)
  between operations  16.6 us (2%)
    pallas_call x4, Pallas kernels, plane_sum(): pl.pallas_call(functools.partial(sum_kernel, len(lefts), terms, min(tile,...  155 us
    pallas_call x3, Pallas kernels, plane_gather(): pl.pallas_call(gather_kernel, out_shape=jax.ShapeDtypeStruct((8, *value.s...  93.4 us
    all_gather x2, waiting for transfers between devices, over_planes(): lax.all_gather(blocks.reshape(-1, blocks.shape[-1]), 'z', axis=0, tiled=T...  90.1 us
    pallas_call x1, Pallas kernels, begin(): pl.pallas_call(functools.partial(begin_kernel, planes, *takes), out_shape...  71.3 us
    dot_general x7, matrix products, dot(): lax.dot_general(left, right, (contract, ((), ())), preferred_element_type...  63.6 us
    pallas_call x1, Pallas kernels, fall(): pl.pallas_call(functools.partial(fall_kernel, planes), out_shape=[jax.Sha...  44 us
    pallas_call x2, Pallas kernels, turn(): pl.pallas_call(functools.partial(turn_kernel, planes), out_shape=out_shap...  29.6 us
    pallas_call x2, Pallas kernels, attention_call(): pl.pallas_call(kernel, grid_spec=pltpu.PrefetchScalarGridSpec(num_scalar_...  25.6 us
  transfers between devices with their start and end apart: 6, of which 4 were waited for; matrix products, arithmetic and copies ran while one was open for 12% of the time, Pallas kernels for 46%

commit v1 on v0

--- a/solution.py
+++ b/solution.py
@@ -773,11 +773,12 @@
     def rows_of(member):
         return rows.at[pl.ds(pl.multiple_of(member * count, count), count)]
 
-    half = terms.shape[1] // 2
-    parts = [pl.ds(n * half, half) for n in range(2)]
+    pieces = 3
+    third = terms.shape[1] // pieces
+    parts = [pl.ds(n * third, third) for n in range(pieces)]
 
     def hop(step, n):
-        slot = 2 * (step - 1) + n
+        slot = pieces * (step - 1) + n
         return pltpu.make_async_remote_copy(
             src_ref=sends.at[step - 1, parts[n]], dst_ref=recvs.at[step - 1, parts[n]],
             send_sem=send.at[slot], recv_sem=recv.at[slot], device_id={"z": z - 1}, device_id_type=MESH,
@@ -797,7 +798,7 @@
     pushes = []
     for step in range(1, planes):
         block = z + step - planes
-        for n in range(2):
+        for n in range(pieces):
             lines = parts[n]
             if step > 1:
                 pl.when(came(step - 1))(lambda: hop(step - 1, n).wait_recv())
@@ -827,7 +828,7 @@
     last = planes - 1
     sides, span = cos.shape[:2]
     get_left.wait()
-    for n in range(2):
+    for n in range(pieces):
         lines = parts[n]
 
         @pl.when(came(last))
@@ -835,7 +836,7 @@
             hop(last, n).wait_recv()
             total[lines] += recvs[last - 1, lines].astype(f32)
 
-        for line in range(n * half, (n + 1) * half, span):
+        for line in range(n * third, (n + 1) * third, span):
             side = line // (total.shape[0] // sides)
             part = total[line : line + span]
             part = jnp.where(c == 0, turned(part, cos[side], -sin[side]), part)
@@ -844,10 +845,12 @@
         for start in range(0, left.shape[1], 512):
             columns = pl.ds(start, 512)
             made = mm(upright, left[lines, columns])
-            if n == 0:
+            if n > 0:
+                made += first[:, columns]
+            if n < pieces - 1:
                 first[:, columns] = made
                 continue
-            held[2, columns] = (first[:, columns] + made).T.astype(held.dtype)
+            held[2, columns] = made.T.astype(held.dtype)
             pushes.append(
                 pltpu.make_async_copy(
                     held.at[2, columns], term.at[columns, pl.ds(size, size)], move.at[4 + start // 512]
@@ -855,7 +858,7 @@
             )
             pushes[-1].start()
     for step in range(1, planes):
-        for n in range(2):
+        for n in range(pieces):
             pl.when(z + step - planes >= 0)(lambda: hop(step, n).wait_send())
     for copy in copies + pushes:
         copy.wait()
@@ -877,7 +880,7 @@
         + [pltpu.VMEM((planes - 1, *block), low)] * 2
         + [pltpu.VMEM(block, jnp.float32), pltpu.VMEM((block[1], left.shape[1]), jnp.float32)]
         + [pltpu.VMEM((3, left.shape[1], block[1]), low)]
-        + [dma((2 * (planes - 1),))] * 2
+        + [dma((3 * (planes - 1),))] * 2
         + [dma((7,)), dma((7,)), dma, dma((4 + left.shape[1] // 512,)), dma((2,))],
         compiler_params=pltpu.CompilerParams(
             collective_id=number, has_side_effects=True, vmem_limit_bytes=56 * 2**20
@@ -1312,7 +1315,7 @@
         attention_term = jnp.concatenate([query_term, mm_tn(h1, dkv).astype(low), out_term], axis=1)
         gate_up_grad = scatter_team(gate_up_rows, 8)
     attention_rows = scatter_planes(attention_term)
-    dh1 = team_sum([dq, dkv], [query_weight, kv_weight], 9, [attention_term])
+    dh1 = team_sum([dq, dkv], [query_weight, kv_weight], 9)
     in_grad, gain_one = rms_back(dh1, x_in, inverse_one, norm_gains[0])
     input_gradient = dr + in_grad
     gain_local = jnp.stack([gain_one, gain_two]).reshape(-1, 128)

time: 768 us -> 768 us (level)
  no operation moved by 1% of the time
where the time goes in v1:
time: 768 us; the launch traced here: 760 us
  Pallas kernels  520 us (68%)
  waiting for transfers between devices  104 us (14%)
  matrix products  63.6 us (8%)
  other arithmetic  24.1 us (3%)
  local copies, waits for them, and re-layouts  23.7 us (3%)
  between operations  16.6 us (2%)
    pallas_call x4, Pallas kernels, plane_sum(): pl.pallas_call(functools.partial(sum_kernel, len(lefts), terms, min(tile,...  155 us
    pallas_call x3, Pallas kernels, plane_gather(): pl.pallas_call(gather_kernel, out_shape=jax.ShapeDtypeStruct((8, *value.s...  93.4 us
    all_gather x2, waiting for transfers between devices, over_planes(): lax.all_gather(blocks.reshape(-1, blocks.shape[-1]), 'z', axis=0, tiled=T...  90.1 us
    pallas_call x1, Pallas kernels, begin(): pl.pallas_call(functools.partial(begin_kernel, planes, *takes), out_shape...  71.3 us
    dot_general x7, matrix products, dot(): lax.dot_general(left, right, (contract, ((), ())), preferred_element_type...  63.6 us
    pallas_call x1, Pallas kernels, fall(): pl.pallas_call(functools.partial(fall_kernel, planes), out_shape=[jax.Sha...  38.2 us
    pallas_call x1, Pallas kernels, total_sum(): pl.pallas_call(functools.partial(total_kernel, planes), out_shape=jax.Sha...  30.7 us
    pallas_call x2, Pallas kernels, turn(): pl.pallas_call(functools.partial(turn_kernel, planes), out_shape=out_shap...  29.6 us
  transfers between devices with their start and end apart: 6, of which 4 were waited for; matrix products, arithmetic and copies ran while one was open for 12% of the time, Pallas kernels for 46%

profile of v1, /device:TPU:1, one launch (start us, length us, event | category | flops | bytes accessed | tf_op | source)
XLA Modules:
  0.0 759.7 jit_solution(2703604523681108474)
XLA Ops:
  9.6 71.3 %begin.1 = (bf16[2048,768]{1,0:T(8,128)(2,1)}, bf16[8,192,2048]{2,1,0:T(8,128)(2,1)}, bf16[8,64,2048]{2,1,0:T(8,128)(2,1)}) custom-call(f32[64,6144]{1,0:T(8,128)} %refs_12_.1, f32[64,24576]{1,0:T(8,128)} %refs_9_.1, bf16[192,2048]{1,0:T(8,128)(2,1)} %bitcast.61, f32[1,2048]{1,0:T(1,128)} %get-tuple-element.100.gain), custom_call_target="tpu_custom_call" | custom-call | flops 1 | bytes 1 | tf_op jit(solution)/shard_map/begin/pallas_call | solution.py:604
  80.9 21.6 %climb.1 = (bf16[4,1536,256]{2,1,0:T(8,128)(2,1)}, bf16[4,1536,256]{2,1,0:T(8,128)(2,1)}) custom-call(bf16[1536,2048]{1,0:T(8,128)(2,1)} %bitcast.67, bf16[2048,768]{1,0:T(8,128)(2,1)} %get-tuple-element.51.weights, f32[2,64,128]{2,1,0:T(8,128)} %get-tuple-element.101.cos, f32[2,64,128]{2,1,0:T(8,128)} %get-tuple-element.102.sin), custom_call_target="tpu_custom_call" | custom-call | flops 1 | bytes 1 | tf_op jit(solution)/shard_map/climb/pallas_call | solution.py:727
  117.7 10.5 %attention.3 = bf16[2,12,64,256]{3,2,1,0:T(8,128)(2,1)S(1)} custom-call(s32[5]{0:T(128)S(1)} %pad_add_fusion.1.core_ref, s32[12]{0:T(128)S(1)} %all-reduce.1.length_ref, bf16[2,12,64,256]{3,2,1,0:T(8,128)(2,1)S(1)} %pad_maximum_fusion.q_ref, bf16[4,2,12,64,256]{4,3,2,1,0:T(8,128)(2,1)S(1)} %bitcast.49, bf16[4,2,12,64,256]{4,3,2,1,0:T(8,128)(2,1)} %bitcast.73, ...), custom_call_target="tpu_custom_call" | custom-call | flops 1 | bytes 1 | tf_op jit(solution)/shard_map/attention/pallas_call | solution.py:1002
  129.8 33.4 %plane_sum.4 = f32[192,2048]{1,0:T(8,128)S(1)} custom-call(bf16[1536,256]{1,0:T(8,128)(2,1)S(1)} %bitcast.50, bf16[2048,256]{1,0:T(8,128)(2,1)S(1)} %get-tuple-element.95.refs_1_), custom_call_target="tpu_custom_call" | custom-call | flops 1 | bytes 1 | tf_op jit(solution)/shard_map/plane_sum/pallas_call | solution.py:214
  165.7 31.1 %plane_gather.3 = bf16[8,192,2048]{2,1,0:T(8,128)(2,1)} custom-call(bf16[192,2048]{1,0:T(8,128)(2,1)} %multiply_convert_fusion.src), custom_call_target="tpu_custom_call" | custom-call | flops 1 | bytes 1 | tf_op jit(solution)/shard_map/plane_gather/pallas_call | solution.py:108
  198.1 31.1 %plane_gather.4 = bf16[8,192,2048]{2,1,0:T(8,128)(2,1)} custom-call(bf16[192,2048]{1,0:T(8,128)(2,1)} %fusion.10.src, bf16[1536,2048]{1,0:T(8,128)(2,1)} %bitcast.64), custom_call_target="tpu_custom_call" | custom-call | flops 1 | bytes 1 | tf_op jit(solution)/shard_map/plane_gather/pallas_call | solution.py:108
  229.2 17.8 %plane_swap.1 = bf16[8,64,1024]{2,1,0:T(8,128)(2,1)} custom-call(f32[64,24576]{1,0:T(8,128)} %refs_9_.1, bf16[1536,2048]{1,0:T(8,128)(2,1)} %bitcast.57), custom_call_target="tpu_custom_call" | custom-call | flops 1 | bytes 1 | tf_op jit(solution)/shard_map/plane_swap/pallas_call | solution.py:276
  247.2 43.1 %all-gather.5.cloned.1.call-done.refs_1_ = bf16[2048,2048]{1,0:T(8,128)(2,1)} async-done(((bf16[512,2048]{1,0:T(8,128)(2,1)}), bf16[2048,2048]{1,0:T(8,128)(2,1)}) %all-gather.5.cloned.1.call-update) | async-done | bytes 8388624 | tf_op jit(solution)/shard_map/all_gather | solution.py:1130
  290.3 17.3 %fusion.21.gate_ref.up_ref = f32[1536,2048]{1,0:T(8,128)S(1)} fusion(bf16[1536,2048]{1,0:T(8,128)(2,1)} %bitcast.65, bf16[2048,2048]{1,0:T(8,128)(2,1)} %all-gather.5.cloned.1.call-done.refs_1_), kind=kOutput, calls=%fused_computation.66 | convolution fusion | flops 12884901888 | bytes 27262976 | tf_op jit(solution)/shard_map/dot_general | solution.py:894
  314.9 8.5 %convolution_convert_fusion.1.refs_3_ = bf16[2048,1024]{1,0:T(8,128)(2,1)} fusion(bf16[1536,2048]{1,0:T(8,128)(2,1)S(1)} %bitcast.59, bf16[1536,1024]{1,0:T(8,128)(2,1)S(1)} %fusion.refs_0_), kind=kOutput, calls=%fused_computation.5 | convolution fusion | flops 6444548096 | bytes 13631488 | tf_op jit(solution)/shard_map/dot_general | solution.py:894
  323.7 47.0 %all-gather.3.cloned.1.call-done.weight_ref.refs_1_ = bf16[2048,1024]{1,0:T(8,128)(2,1)} async-done(((bf16[512,1024]{1,0:T(8,128)(2,1)}), bf16[2048,1024]{1,0:T(8,128)(2,1)}) %all-gather.3.cloned.1.call-update) | async-done | bytes 4194320 | tf_op jit(solution)/shard_map/all_gather | solution.py:1130
  372.9 14.0 %feed_back.1.refs_0_ = bf16[1536,2048]{1,0:T(8,128)(2,1)} custom-call(bf16[1536,2048]{1,0:T(8,128)(2,1)} %bitcast.58, bf16[2048,1024]{1,0:T(8,128)(2,1)S(1)} %copy-done, f32[1536,2048]{1,0:T(8,128)} %copy-done.13, f32[1536,2048]{1,0:T(8,128)} %copy-done.13), custom_call_target="tpu_custom_call" | custom-call | flops 1 | bytes 1 | tf_op jit(solution)/shard_map/feed_back/pallas_call | solution.py:1033
  386.9 19.4 %convolution_convert_fusion.refs_2_ = bf16[2048,2048]{1,0:T(8,128)(2,1)} fusion(bf16[1536,2048]{1,0:T(8,128)(2,1)} %bitcast.66, bf16[1536,2048]{1,0:T(8,128)(2,1)} %feed_back.1.refs_0_), kind=kOutput, calls=%fused_computation | convolution fusion | flops 12889096192 | bytes 20971520 | tf_op jit(solution)/shard_map/dot_general | solution.py:894
  409.4 49.1 %plane_sum.5 = f32[192,2048]{1,0:T(8,128)S(1)} custom-call(bf16[1536,2048]{1,0:T(8,128)(2,1)} %feed_back.1.refs_0_, bf16[2048,2048]{1,0:T(8,128)(2,1)} %all-gather.5.cloned.1.call-done.refs_1_, bf16[2048,2048]{1,0:T(8,128)(2,1)} %convolution_convert_fusion.refs_2_, bf16[2048,1024]{1,0:T(8,128)(2,1)S(1)} %copy-done.1), custom_call_target="tpu_custom_call" | custom-call | flops 1 | bytes 1 | tf_op jit(solution)/shard_map/plane_sum/pallas_call | solution.py:214
  461.8 31.2 %plane_gather.5 = bf16[8,192,2048]{2,1,0:T(8,128)(2,1)} custom-call(bf16[192,2048]{1,0:T(8,128)(2,1)} %get-tuple-element.90.src, bf16[512,1024]{1,0:T(8,128)(2,1)} %reduce-scatter.4.cloned.1.call-done.refs_0_.src), custom_call_target="tpu_custom_call" | custom-call | flops 1 | bytes 1 | tf_op jit(solution)/shard_map/plane_gather/pallas_call | solution.py:108
  497.9 15.1 %attention_back.1 = (bf16[2,12,64,256]{3,2,1,0:T(8,128)(2,1)S(1)}, f32[4,2,12,64,256]{4,3,2,1,0:T(8,128)}, bf16[4,2,12,64,256]{4,3,2,1,0:T(8,128)(2,1)S(1)}) custom-call(s32[5]{0:T(128)S(1)} %pad_add_fusion.1.core_ref, s32[12]{0:T(128)S(1)} %all-reduce.1.length_ref, bf16[2,12,64,256]{3,2,1,0:T(8,128)(2,1)S(1)} %copy-done.4, ...), custom_call_target="tpu_custom_call" | custom-call | flops 1 | bytes 1 | tf_op jit(solution)/shard_map/attention_back/pallas_call | solution.py:1002
  528.8 37.4 %plane_sum.6 = f32[192,2048]{1,0:T(8,128)S(1)} custom-call(bf16[1536,1024]{1,0:T(8,128)(2,1)S(1)} %fusion.refs_0_, bf16[2048,1024]{1,0:T(8,128)(2,1)} %all-gather.3.cloned.1.call-done.weight_ref.refs_1_, bf16[4,2,12,64,256]{4,3,2,1,0:T(8,128)(2,1)} %add_convert_fusion.refs_2_.refs_0_), custom_call_target="tpu_custom_call" | custom-call | flops 1 | bytes 1 | tf_op jit(solution)/shard_map/plane_sum/pallas_call | solution.py:214
  566.2 15.1 %turn.2.refs_4_ = bf16[8,64,1024]{2,1,0:T(8,128)(2,1)} custom-call(bf16[512,1024]{1,0:T(8,128)(2,1)} %reduce-scatter.4.cloned.1.call-done.refs_0_.src, bf16[4,2,12,64,256]{4,3,2,1,0:T(8,128)(2,1)} %add_convert_fusion.refs_2_.refs_0_), custom_call_target="tpu_custom_call" | custom-call | flops 1 | bytes 1 | tf_op jit(solution)/shard_map/turn/pallas_call | solution.py:432
  582.4 13.7 %reduce-scatter.6.cloned.1.call-done.rows = bf16[512,2048]{1,0:T(8,128)(2,1)} async-done(((bf16[2048,2048]{1,0:T(8,128)(2,1)}), bf16[512,2048]{1,0:T(8,128)(2,1)}) %reduce-scatter.6.cloned.1.call-update) | async-done | bytes 2097168 | tf_op jit(solution)/shard_map/reduce_scatter | solution.py:1134
  596.1 38.2 %fall.1 = (bf16[1536,256]{1,0:T(8,128)(2,1)}, bf16[2048,768]{1,0:T(8,128)(2,1)}, bf16[8,64,2048]{2,1,0:T(8,128)(2,1)}) custom-call(bf16[4,1536,256]{2,1,0:T(8,128)(2,1)} %bitcast.60, bf16[512,2048]{1,0:T(8,128)(2,1)} %reduce-scatter.6.cloned.1.call-done.rows, bf16[1536,2048]{1,0:T(8,128)(2,1)} %bitcast.69, ...), custom_call_target="tpu_custom_call" | custom-call | flops 1 | bytes 1 | tf_op jit(solution)/shard_map/fall/pallas_call | solution.py:870
  640.5 35.5 %plane_sum.7 = f32[192,2048]{1,0:T(8,128)S(1)} custom-call(bf16[1536,256]{1,0:T(8,128)(2,1)S(1)} %bitcast.53, bf16[1536,256]{1,0:T(8,128)(2,1)S(1)} %copy-done.11, bf16[2048,256]{1,0:T(8,128)(2,1)S(1)} %copy-done.6, bf16[2048,256]{1,0:T(8,128)(2,1)S(1)} %copy-done.5), custom_call_target="tpu_custom_call" | custom-call | flops 1 | bytes 1 | tf_op jit(solution)/shard_map/plane_sum/pallas_call | solution.py:214
  681.1 30.7 %total_sum.1.refs_0_ = f32[40,128]{1,0:T(8,128)S(1)} custom-call(f32[40,128]{1,0:T(8,128)S(1)} %concatenate.16.src), custom_call_target="tpu_custom_call" | custom-call | flops 1 | bytes 1 | tf_op jit(solution)/shard_map/total_sum/pallas_call | solution.py:406
  716.0 14.4 %turn.3 = (bf16[8,64,768]{2,1,0:T(8,128)(2,1)}, f32[8,128]{1,0:T(8,128)}) custom-call(bf16[512,768]{1,0:T(8,128)(2,1)} %reduce-scatter.8.cloned.1.call-done.src), custom_call_target="tpu_custom_call" | custom-call | flops 1 | bytes 1 | tf_op jit(solution)/shard_map/turn/pallas_call | solution.py:432
  730.5 22.4 %update.1 = (f32[2,2048]{1,0:T(2,128)}, f32[2,2048]{1,0:T(2,128)}, f32[2,2048]{1,0:T(2,128)}, f32[1,1]{1,0:T(1,128)}, f32[64,24576]{1,0:T(8,128)}, /*index=5*/f3...) custom-call(f32[40,128]{1,0:T(8,128)} %copy-done.12, ...), custom_call_target="tpu_custom_call" | custom-call | tf_op jit(solution)/shard_map/update/pallas_call | solution.py:1109
  (132 shorter events, 74.4 us)
Async XLA Ops:
  7.2 283.2 %all-gather.5.cloned.1.call-start = ((), (), s32[]{:S(2)}) async-start(), calls=%async_computation.4 | async-start | bytes 10485760 | tf_op jit(solution)/shard_map/all_gather | solution.py:1130
  80.9 30.0 %copy-start.22 = (bf16[2048,768]{1,0:T(8,128)(2,1)S(1)}, bf16[2048,768]{1,0:T(8,128)(2,1)}, u32[]{:S(2)}) copy-start(bf16[2048,768]{1,0:T(8,128)(2,1)} %get-tuple-element.51.weights) | copy-start | bytes 9437188
  102.6 268.2 %all-gather.3.cloned.1.call-start = ((), (), s32[]{:S(2)}) async-start(), calls=%async_computation.3 | async-start | bytes 5242880 | tf_op jit(solution)/shard_map/all_gather | solution.py:1130
  110.9 4.7 copy-start.27
  110.9 4.6 copy-start.28
  115.9 12.3 %copy-start.3 = (bf16[2,12,64,256]{3,2,1,0:T(8,128)(2,1)}, bf16[2,12,64,256]{3,2,1,0:T(8,128)(2,1)S(1)}, u32[]{:S(2)}) copy-start(bf16[2,12,64,256]{3,2,1,0:T(8,128)(2,1)S(1)} %pad_maximum_fusion.q_ref) | copy-start | bytes 2359300
  129.8 33.4 %copy-start.18 = (bf16[3,64,2048]{2,1,0:T(8,128)(2,1)S(1)}, bf16[3,64,2048]{2,1,0:T(8,128)(2,1)}, u32[]{:S(2)}) copy-start(bf16[3,64,2048]{2,1,0:T(8,128)(2,1)} %param.12) | copy-start | bytes 2359300
  165.7 31.3 %copy-start.24 = (bf16[3,64,2048]{2,1,0:T(8,128)(2,1)S(1)}, bf16[3,64,2048]{2,1,0:T(8,128)(2,1)}, u32[]{:S(2)}) copy-start(bf16[3,64,2048]{2,1,0:T(8,128)(2,1)} %param.17) | copy-start | bytes 2359300
  247.0 214.8 %reduce-scatter.4.cloned.1.call-start = ((), (), s32[]{:S(2)}) async-start(), calls=%async_computation.5 | async-start | bytes 5242880 | tf_op jit(solution)/shard_map/reduce_scatter | solution.py:1134
  307.6 4.5 copy-start.13
  323.4 272.7 %reduce-scatter.6.cloned.1.call-start = ((), (), s32[]{:S(2)}) async-start(), calls=%async_computation.6 | async-start | bytes 10485760 | tf_op jit(solution)/shard_map/reduce_scatter | solution.py:1134
  406.3 309.7 %reduce-scatter.8.cloned.1.call-start = ((), (), s32[]{:S(2)}) async-start(), calls=%async_computation.7 | async-start | bytes 3932160 | tf_op jit(solution)/shard_map/reduce_scatter | solution.py:1134
  409.4 49.1 %copy-start.16 = (f32[192,2048]{1,0:T(8,128)S(1)}, f32[192,2048]{1,0:T(8,128)}, u32[]{:S(2)}) copy-start(f32[192,2048]{1,0:T(8,128)} %copy-done.15) | copy-start | bytes 4718596
  493.0 4.9 copy-start.4
  497.9 15.4 %copy-start.8 = (bf16[2,12,64,256]{3,2,1,0:T(8,128)(2,1)S(1)}, bf16[2,12,64,256]{3,2,1,0:T(8,128)(2,1)}, u32[]{:S(2)}) copy-start(bf16[2,12,64,256]{3,2,1,0:T(8,128)(2,1)} %copy-done.7) | copy-start | bytes 2359300
  497.9 28.0 %slice-start = ((s8[6291456]{0:T(1024)(128)(4,1)}), s8[4194304]{0:T(1024)(128)(4,1)S(1)}, s32[]{:S(2)}) async-start(s8[6291456]{0:T(1024)(128)(4,1)} %bitcast.70), calls=%async_computation.8 | async-start | bytes 8388608
  513.1 12.8 %copy-start.9 = (bf16[2,12,64,256]{3,2,1,0:T(8,128)(2,1)}, bf16[2,12,64,256]{3,2,1,0:T(8,128)(2,1)S(1)}, u32[]{:S(2)}) copy-start(bf16[2,12,64,256]{3,2,1,0:T(8,128)(2,1)S(1)} %get-tuple-element.62) | copy-start | bytes 2359300
  513.1 12.8 %slice-start.1 = ((s8[6291456]{0:T(1024)(128)(4,1)}), s8[2097152]{0:T(1024)(128)(4,1)S(1)}, s32[]{:S(2)}) async-start(s8[6291456]{0:T(1024)(128)(4,1)} %bitcast.70), calls=%async_computation.9 | async-start | bytes 4194304
  513.1 6.3 collective-permute-start
  513.3 7.7 %copy-start.23 = (f32[4,2,12,64,256]{4,3,2,1,0:T(8,128)S(1)}, f32[4,2,12,64,256]{4,3,2,1,0:T(8,128)}, u32[]{:S(2)}) copy-start(f32[4,2,12,64,256]{4,3,2,1,0:T(8,128)} %get-tuple-element.60) | copy-start | bytes 18874372
  566.2 15.2 %copy-start.17 = (f32[192,2048]{1,0:T(8,128)S(1)}, f32[192,2048]{1,0:T(8,128)}, u32[]{:S(2)}) copy-start(f32[192,2048]{1,0:T(8,128)} %copy-done.15) | copy-start | bytes 4718596
  640.5 35.5 %copy-start.20 = (bf16[3,64,2048]{2,1,0:T(8,128)(2,1)S(1)}, bf16[3,64,2048]{2,1,0:T(8,128)(2,1)}, u32[]{:S(2)}) copy-start(bf16[3,64,2048]{2,1,0:T(8,128)(2,1)} %param.12) | copy-start | bytes 2359300
  640.5 35.5 %copy-start.29 = (f32[1,2048]{1,0:T(1,128)S(1)}, f32[1,2048]{1,0:T(1,128)}, u32[]{:S(2)}) copy-start(f32[1,2048]{1,0:T(1,128)} %get-tuple-element.100.gain) | copy-start | bytes 24580
  676.0 36.4 %copy-start.21 = (bf16[3,64,2048]{2,1,0:T(8,128)(2,1)S(1)}, bf16[3,64,2048]{2,1,0:T(8,128)(2,1)}, u32[]{:S(2)}) copy-start(bf16[3,64,2048]{2,1,0:T(8,128)(2,1)} %param.12) | copy-start | bytes 2359300
  (16 other events, 32.4 us)
Sparse Core Ops, SparseCore 0:
  102.7 187.6 all-gather.4
  291.9 78.7 all-gather.2
  373.6 75.2 reduce-scatter.3
  451.3 144.7 reduce-scatter.5
  634.5 81.5 reduce-scatter.7
